TPU v7x, 128 devices: a whole 4x4x4 slice. The times are simulated.
128 devices in a mesh: tm: 128 (over z, x, y, core).
Axes of the slice: x: 4, y: 4, z: 4, core: 2. Of those that a mesh axis runs over, the one named last changes fastest.
Arguments:
- transitions: float32 [1024, 256, 256], P('tm'), may hold values from -1 to 1
- noise_factor: float32 [1024, 256, 256], P('tm'), may hold values from -1 to 1, as said below
- forcing: float32 [1024, 256], P('tm'), may hold values from -0.3125 to 0.3125
- initial_mean: float32 [256], replicated, may hold values from -6 to 6
- initial_factor: float32 [256, 256], replicated, may hold values from -2 to 2, as said below
Outputs:
- means: float32 [1024, 256], P('tm')
- factors: float32 [1024, 256, 256], P('tm')
- log_scale: float32 [], replicated
Inputs may be any that keep to these rules, and one draw needn't show every extreme that they name: `noise_factor`: each matrix is lower triangular with a positive diagonal. `initial_factor`: lower triangular with a positive diagonal.
All inputs are finite; a program needn't handle non-finite values.
Results may differ from a plain program's by a relative error of at most 0.0003.
Values sent between devices are 32-bit elements; how exact they have to be, the bound alone decides.
No kernel may reach another device: no remote copies, remote signals or barrier semaphores. Data moves between devices by JAX's collectives and lax.ppermute only.
A program may use at most 192 MiB of HBM per device.

v0:
```python
import jax
import jax.numpy as jnp
from jax import lax
from jax.experimental import pallas as pl
from jax.experimental.pallas import tpu as pltpu
from jax.sharding import Mesh, PartitionSpec as P

f32, bf16 = jnp.float32, jnp.bfloat16
AXES = ("z", "x", "y", "c")
N = 256
H = 128
STEPS = 8
ROWS = 400
HALF = ROWS // 2
PB = 8
NB = 32


def split(x):
    hi = x.astype(bf16)
    return hi, (x - hi.astype(f32)).astype(bf16)


def dg(a, b, ca, cb):
    return lax.dot_general(a, b, (((ca,), (cb,)), ((), ())), preferred_element_type=f32)


def mm3(a, b, ca=1, cb=0):
    return dg(a[0], b[0], ca, cb) + (dg(a[0], b[1], ca, cb) + dg(a[1], b[0], ca, cb))


def mm4(a, b):
    return dg(a[0], b[0], 1, 0) + ((dg(a[0], b[1], 1, 0) + dg(a[1], b[0], 1, 0)) + dg(a[1], b[1], 1, 0))


def through(a, cov, b):
    high, low = split(mm3(a, cov))
    wide = jnp.concatenate([b, b], axis=0)
    v1 = wide.astype(bf16)
    rest = wide - v1.astype(f32)
    v2 = rest.astype(bf16)
    v3 = (rest - v2.astype(f32)).astype(bf16)
    by_high = dg(jnp.concatenate([high, low, v1, v2, v3], axis=0), a[0], 1, 1)
    by_low = dg(jnp.concatenate([high, v1, v2], axis=0), a[1], 1, 1)
    out = by_high[:N] + (by_high[N : 2 * N] + by_low[:N])
    vec = by_high[2 * N + 32 : 2 * N + 40] + by_low[N + 16 : N + 24]
    vec = vec + (by_high[2 * N + 16 : 2 * N + 24] + by_low[N : N + 8])
    return out, by_high[2 * N : 2 * N + 8] + vec


def grid_iota():
    return (
        lax.broadcasted_iota(jnp.int32, (H, H), 0),
        lax.broadcasted_iota(jnp.int32, (H, H), 1),
    )


def pack(out, a, p, b):
    r, c = grid_iota()
    out[0:N, :] = a
    out[N : N + H, 0:H] = p[H:, :H]
    out[N : N + H, H:] = jnp.where(r >= c, p[:H, :H], p[H:, H:])
    diag = jnp.sum(jnp.where(r == c, p[H:, H:], 0.0), axis=0, keepdims=True)
    row = lax.broadcasted_iota(jnp.int32, (8, N), 0)
    wide = jnp.concatenate([diag, diag], axis=1)
    out[N + H : N + H + 8, :] = jnp.where(row == 0, b, jnp.broadcast_to(wide, (8, N)))
    out[N + H + 8 :, :] = jnp.zeros((8, N), f32)


def unpack(ref):
    r, c = grid_iota()
    a = ref[0:N, :]
    x = ref[N : N + H, H:]
    tail = ref[N + H : N + H + 8, :]
    d2 = tail[1:2, :H]
    z11 = jnp.where(r > c, x, jnp.where(r == c, 0.5 * x, 0.0))
    z22 = jnp.where(r < c, x, jnp.where(r == c, 0.5 * jnp.broadcast_to(d2, (H, H)), 0.0))
    top = jnp.concatenate([z11, jnp.zeros((H, H), f32)], axis=1)
    low = jnp.concatenate([ref[N : N + H, :H], z22], axis=1)
    return a, jnp.concatenate([top, low], axis=0), jnp.broadcast_to(tail[0:1, :], (8, N))


class Step:
    def __init__(self, a, cov, b):
        self.a, self.cov, self.b = a, cov, b
        self.a2, self.cov2 = split(a), split(cov)

    def after(self, earlier):
        cov, b = through(self.a2, earlier.cov2, earlier.b)
        return Step(mm4(self.a2, earlier.a2), cov + self.cov, b + self.b)


def apply_to(step, state):
    z, m = through(step.a2, split(state[0]), state[1])
    return z + step.cov, m + step.b


def fetch(t_hbm, n_hbm, f_hbm, t_buf, n_buf, f_buf, sems, f_sem):
    copies = []
    pushes = pltpu.make_async_copy(f_hbm, f_buf, f_sem)
    pushes.start()
    for k in range(STEPS):
        pair = [
            pltpu.make_async_copy(n_hbm.at[k], n_buf.at[k], sems.at[k, 0]),
            pltpu.make_async_copy(t_hbm.at[k], t_buf.at[k], sems.at[k, 1]),
        ]
        for copy in pair:
            copy.start()
        copies.append(pair)

    pushes.wait()

    def one(k):
        for copy in copies[k]:
            copy.wait()
        noise = split(n_buf[k])
        push = jnp.broadcast_to(f_buf[k : k + 1, :], (8, N))
        return Step(t_buf[k], mm3(noise, noise, 1, 1), push)

    return one


def local_kernel(t_hbm, n_hbm, f_hbm, total, *buffers):
    one = fetch(t_hbm, n_hbm, f_hbm, *buffers)
    pairs = []
    for k in range(0, STEPS, 2):
        earlier, later = one(k), one(k + 1)
        pairs.append(later.after(earlier))
    whole = pairs[3].after(pairs[2]).after(pairs[1].after(pairs[0]))
    pack(total, whole.a, whole.cov, whole.b)


def prefix_kernel(t_hbm, n_hbm, f_hbm, later, a_out, p_out, b_out, *buffers):
    one = fetch(t_hbm, n_hbm, f_hbm, *buffers)

    def put(k, step):
        a_out[k], p_out[k], b_out[k] = step.a, step.cov, step.b

    g, pairs = [], []
    for k in range(0, STEPS, 2):
        g += [one(k), one(k + 1)]
        pairs.append(g[k + 1].after(g[k]))
    put(0, g[0])
    put(1, pairs[0])
    put(2, g[2].after(pairs[0]))
    front = pairs[1].after(pairs[0])
    put(3, front)
    put(4, g[4].after(front))
    six = pairs[2].after(front)
    put(5, six)
    put(6, g[6].after(six))
    put(7, pairs[3].after(six))


def take_half(half, whole, c):
    half[...] = whole[pl.ds(pl.multiple_of(c * HALF, 8), HALF), :]


def core_kernel(place, own, other, half, total):
    c = place[3]
    mine, theirs = unpack(own), unpack(other)
    earlier = Step(*[jnp.where(c == 0, u, v) for u, v in zip(mine, theirs)])
    later = Step(*[jnp.where(c == 0, v, u) for u, v in zip(mine, theirs)])
    both = later.after(earlier)
    pack(total, both.a, both.cov + both.cov.T, both.b)
    take_half(half, total, c)


def stack_kernel(r1, r2, r3, beside, out):
    for k, r in enumerate((r1, r2, r3)):
        out[k] = r[...]


def lay_out(pieces, place, which, direct, passed):
    me, c = place[which], place[3]
    here = pl.multiple_of(c * HALF, 8)
    there = pl.multiple_of((1 - c) * HALF, 8)
    for back in (1, 2, 3):
        spot = lax.rem(me + 4 - back, 4)
        pieces[spot, pl.ds(here, HALF), :] = direct[back - 1]
        pieces[spot, pl.ds(there, HALF), :] = passed[back - 1]


def neutral():
    rows = lax.broadcasted_iota(jnp.int32, (N, N), 0)
    columns = lax.broadcasted_iota(jnp.int32, (N, N), 1)
    eye = jnp.where(rows == columns, 1.0, 0.0)
    return eye, jnp.zeros((N, N), f32), jnp.zeros((8, N), f32)


def ring_kernel(which, place, own, direct, passed, half, total, pieces):
    pieces[place[which]] = own[...]
    lay_out(pieces, place, which, direct, passed)
    g = [Step(*unpack(pieces.at[k])) for k in range(4)]
    whole = g[3].after(g[2]).after(g[1].after(g[0]))
    pack(total, whole.a, whole.cov + whole.cov.T, whole.b)
    take_half(half, total, place[3])


def members_before(pieces, place, which, direct, passed, ea, ez, eb):
    lay_out(pieces, place, which, direct, passed)
    me = place[which]
    ea[...], ez[...], eb[...] = neutral()

    def one(k, _):
        step = Step(*unpack(pieces.at[k])).after(Step(ea[...], ez[...], eb[...]))
        ea[...], ez[...], eb[...] = step.a, step.cov, step.b
        return 0

    lax.fori_loop(0, me, one, 0)


def before_y_kernel(place, direct, passed, later, ea, ez, eb, pieces):
    members_before(pieces, place, 2, direct, passed, ea, ez, eb)


def entry_kernel(place, direct, passed, ya, yz, yb, core, ea, ez, eb, pieces):
    members_before(pieces, place, 1, direct, passed, ea, ez, eb)
    c = place[3]
    last = Step(*[jnp.where(c == 1, u, v) for u, v in zip(unpack(core), neutral())])
    both = last.after(Step(ya[...], yz[...], yb[...])).after(Step(ea[...], ez[...], eb[...]))
    ea[...], ez[...], eb[...] = both.a, both.cov, both.b


def lane(x, i):
    return jnp.broadcast_to(x[:, i : i + 1], x.shape)


def factor_block(rows, o):
    tiles, count = len(rows), len(rows[0])
    for q in range(0, count, PB):
        a = {(t, s): lane(rows[0][q + t], o + q + s) for t in range(PB) for s in range(t, PB)}
        for t in range(PB):
            inv = lax.rsqrt(a[t, t])
            u = {s: a[t, s] * inv for s in range(t + 1, PB)}
            for s in range(t + 1, PB):
                for r in range(s, PB):
                    a[s, r] = a[s, r] - u[s] * u[r]
            for w in range(tiles):
                rows[w][q + t] = rows[w][q + t] * inv
                for s in range(t + 1, PB):
                    rows[w][q + s] = rows[w][q + s] - u[s] * rows[w][q + t]
        for i in range(q + PB, count):
            for t in range(PB):
                c = lane(rows[0][q + t], o + i)
                for w in range(tiles):
                    rows[w][i] = rows[w][i] - c * rows[w][q + t]


def strided(j, count, m):
    return pl.ds(STEPS * j + m, count, stride=STEPS)


def cholesky(cov, l_ref, logs_ref, u0, u1):
    us = (u0, u1)
    for j0 in range(0, N, NB):
        first, r0 = j0 // H, j0 + NB
        tiles = range(first, 2)
        for m in range(STEPS):
            for w in tiles:
                us[w][strided(j0, NB, m), :] = cov[m, j0:r0, H * w : H * w + H]
        rows = [[us[w][pl.ds(8 * (j0 + i), 8), :] for i in range(NB)] for w in tiles]
        factor_block(rows, j0 % H)
        for w in tiles:
            for i in range(NB):
                us[w][pl.ds(8 * (j0 + i), 8), :] = rows[w - first][i]
        if r0 == N:
            break
        for m in range(STEPS):
            u = jnp.concatenate([us[w][strided(j0, NB, m), :] for w in tiles], axis=1)
            left, right = split(u.T[r0 - H * first :, :]), split(u)
            cov[m, r0:, H * first :] = cov[m, r0:, H * first :] - mm3(left, right)
    r, c = grid_iota()
    diagonals = []
    for m in range(STEPS):
        a1 = u0[strided(0, H, m), :]
        a2 = u1[strided(H, H, m), :]
        diagonals += [jnp.sum(jnp.where(r == c, u, 0.0), axis=0, keepdims=True) for u in (a1, a2)]
        l_ref[m, 0:H, 0:H] = jnp.where(r <= c, a1, 0.0).T
        l_ref[m, H:, 0:H] = u1[strided(0, H, m), :].T
        l_ref[m, H:, H:] = jnp.where(r <= c, a2, 0.0).T
        l_ref[m, 0:H, H:] = jnp.zeros((H, H), f32)
    logs = jnp.sum(jnp.log(jnp.concatenate(diagonals, axis=0)), axis=0, keepdims=True)
    logs_ref[...] = jnp.broadcast_to(jnp.sum(logs, axis=1, keepdims=True), (1, H))


def final_kernel(place, direct, passed, ea, ez, eb, a_ref, p_ref, b_ref, m0_ref, l0_ref,
                 means, l_ref, logs, pieces, zs, ms, cov, u0, u1):
    lay_out(pieces, place, 0, direct, passed)
    l0 = split(l0_ref[...])
    zs[...] = 0.5 * mm3(l0, l0, 1, 1)
    ms[...] = jnp.broadcast_to(m0_ref[...], (8, N))

    def slab(k, _):
        zs[...], ms[...] = apply_to(Step(*unpack(pieces.at[k])), (zs[...], ms[...]))
        return 0

    lax.fori_loop(0, place[0], slab, 0)
    z, mean = apply_to(Step(ea[...], ez[...], eb[...]), (zs[...], ms[...]))
    state = split(z + z.T)
    for k in range(STEPS):
        spread, moved = through(split(a_ref[k]), state, mean)
        cov[k] = spread + p_ref[k]
        means[k : k + 1, :] = (moved + b_ref[k])[0:1, :]
    cholesky(cov, l_ref, logs, u0, u1)


VMEM = pl.BlockSpec(memory_space=pltpu.VMEM)
ANY = pl.BlockSpec(memory_space=pl.ANY)
HBM = pl.BlockSpec(memory_space=pltpu.HBM)
SMEM = pl.BlockSpec(memory_space=pltpu.SMEM)


def shape(*dims):
    return jax.ShapeDtypeStruct(dims, f32)


def call(kernel, outs, specs, scratch, name, mib, products):
    return pl.pallas_call(
        kernel,
        out_shape=outs,
        in_specs=specs,
        out_specs=(VMEM,) * len(outs),
        scratch_shapes=scratch,
        compiler_params=pltpu.CompilerParams(vmem_limit_bytes=mib * 2**20),
        cost_estimate=pl.CostEstimate(
            flops=products * 6 * N**3, bytes_accessed=8 * N * N * products, transcendentals=0
        ),
        name=name,
    )


def ring(axis, back):
    stride, count = {"c": (1, 2), "y": (2, 4), "x": (8, 4), "z": (32, 4)}[axis]
    pairs = []
    for i in range(128):
        p = (i // stride) % count
        pairs.append((i, i + ((p + back) % count - p) * stride))
    return pairs


def send(x, axis, back):
    return lax.ppermute(x, AXES, ring(axis, back))


def gather_ring(half, axis, beside):
    got = [send(half, axis, back) for back in (1, 2, 3)]
    direct = call(stack_kernel, (shape(3, HALF, N),), [VMEM] * 3 + [ANY], [], "stack_" + axis, 8, 1)(
        *got, beside
    )[0]
    return direct, send(direct, "c", 1)


def on_device(transitions, noise_factor, forcing, initial_mean, initial_factor):
    place = jnp.stack([lax.axis_index(axis) for axis in AXES]).astype(jnp.int32)
    stack = shape(STEPS, N, N)
    packed, half = shape(ROWS, N), shape(HALF, N)
    element = (shape(N, N), shape(N, N), shape(8, N))
    steps_in = [HBM] * 3
    buffers = [
        pltpu.VMEM((STEPS, N, N), f32),
        pltpu.VMEM((STEPS, N, N), f32),
        pltpu.VMEM((STEPS, N), f32),
        pltpu.SemaphoreType.DMA((STEPS, 2)),
        pltpu.SemaphoreType.DMA,
    ]
    lines = [pltpu.VMEM((4, ROWS, N), f32)]
    own = call(local_kernel, (packed,), steps_in, buffers, "local", 52, 29)(
        transitions, noise_factor, forcing
    )[0]
    other = send(own, "c", 1)
    mine, total = call(core_kernel, (half, packed), [SMEM, VMEM, VMEM], [], "core", 16, 3)(
        place, own, other
    )
    a, p, b = call(
        prefix_kernel, (stack, stack, shape(STEPS, 8, N)), steps_in + [ANY], buffers, "prefix", 52, 47
    )(transitions, noise_factor, forcing, total)

    def ring_total(which, axis, got):
        return call(
            lambda *refs: ring_kernel(which, *refs),
            (half, packed),
            [SMEM] + [VMEM] * 3,
            lines,
            "ring_" + axis,
            24,
            9,
        )(place, total, *got)

    along_y = gather_ring(mine, "y", b)
    mine, total = ring_total(2, "y", along_y)
    by_y = call(before_y_kernel, element, [SMEM, VMEM, VMEM, ANY], lines, "before_y", 24, 9)(
        place, *along_y, total
    )
    along_x = gather_ring(mine, "x", by_y[2])
    mine, total = ring_total(1, "x", along_x)
    entry = call(entry_kernel, element, [SMEM] + [VMEM] * 6, lines, "entry", 24, 15)(
        place, *along_x, *by_y, other
    )
    means, factors, logs = call(
        final_kernel,
        (shape(STEPS, N), stack, shape(1, H)),
        [SMEM] + [VMEM] * 10,
        [
            pltpu.VMEM((4, ROWS, N), f32),
            pltpu.VMEM((N, N), f32),
            pltpu.VMEM((8, N), f32),
            pltpu.VMEM((STEPS, N, N), f32),
            pltpu.VMEM((STEPS * N, H), f32),
            pltpu.VMEM((STEPS * N, H), f32),
        ],
        "final",
        48,
        32,
    )(place, *gather_ring(mine, "z", entry[2]), *entry, a, p, b, initial_mean[None], initial_factor)
    logs = lax.all_to_all(logs.reshape(H), AXES, 0, 0, tiled=True)
    log_scale = jnp.sum(logs) / (128 * STEPS * N)
    return means, factors, log_scale


def solution(mesh):
    cube = Mesh(mesh.devices.reshape(4, 4, 4, 2), AXES)
    return jax.shard_map(
        on_device,
        mesh=cube,
        in_specs=(P(AXES, None, None), P(AXES, None, None), P(AXES, None), P(), P()),
        out_specs=(P(AXES, None), P(AXES, None, None), P()),
        check_vma=False,
    )
```

profile of v0, /device:TPU:0, one launch (start us, length us, event | category | flops | bytes accessed | tf_op | source)
XLA Modules:
  0.0 109.4 jit_solution(17300546712218345137)
XLA Ops:
  0.6 0.0 copy-start.1
  0.6 0.7 copy-done.1
  1.3 0.0 copy-start.2
  1.3 6.9 %local.1.own = f32[400,256]{1,0:T(8,128)S(1)} custom-call(f32[8,256,256]{2,1,0:T(8,128)} %t_hbm.3, f32[8,256,256]{2,1,0:T(8,128)} %n_hbm.3, f32[8,256]{1,0:T(8,128)S(1)} %copy-done.1), custom_call_target="tpu_custom_call" | custom-call | flops 2919235584 | bytes 15204352 | tf_op jit(solution)/shard_map/local/pallas_call | solution.py:368
  8.3 0.1 collective-permute-start
  8.4 0.1 pad_add_fusion.place.refs_0_
  8.5 1.6 %collective-permute-done.other.core = f32[400,256]{1,0:T(8,128)S(1)} collective-permute-done((f32[400,256]{1,0:T(8,128)S(1)}, f32[400,256]{1,0:T(8,128)S(1)}, u32[]{:S(2)}, u32[]{:S(2)}) %collective-permute-start) | collective-permute-done | bytes 409632 | tf_op jit(solution)/shard_map/ppermute | solution.py:343
  10.1 1.2 %core.1 = (f32[200,256]{1,0:T(8,128)S(1)}, f32[400,256]{1,0:T(8,128)S(1)}) custom-call(s32[4]{0:T(128)S(1)} %pad_add_fusion.place.refs_0_, f32[400,256]{1,0:T(8,128)S(1)} %local.1.own, f32[400,256]{1,0:T(8,128)S(1)} %collective-permute-done.other.core), custom_call_target="tpu_custom_call" | custom-call | flops 301989888 | bytes 1572864 | tf_op jit(solution)/shard_map/core/pallas_call | solution.py:372
  11.4 3.2 %collective-permute-start.3 = (f32[200,256]{1,0:T(8,128)S(1)}, f32[200,256]{1,0:T(8,128)S(1)}, u32[]{:S(2)}, u32[]{:S(2)}) collective-permute-start(f32[200,256]{1,0:T(8,128)S(1)} %get-tuple-element.21), channel_id=1, source_target_pairs={{0,6},{1,7},{2,0},{3,1},{4,2},{5,3},{6,4},{7,5},{8,14},{9,15},{10,... | collective-permute-start | bytes 614408 | tf_op jit(solution)/shard_map/ppermute | solution.py:343
  14.5 0.6 collective-permute-start.2
  15.2 1.0 collective-permute-start.1
  16.1 0.0 copy-done.2
  16.1 10.6 %prefix.1 = (f32[8,256,256]{2,1,0:T(8,128)}, f32[8,256,256]{2,1,0:T(8,128)}, f32[8,8,256]{2,1,0:T(8,128)S(1)}) custom-call(f32[8,256,256]{2,1,0:T(8,128)} %t_hbm.3, f32[8,256,256]{2,1,0:T(8,128)} %n_hbm.3, f32[8,256]{1,0:T(8,128)S(1)} %copy-done.2, f32[400,256]{1,0:T(8,128)S(1)} %get-tuple-element.20.later.refs_1_), custom_call_target="tpu_custom_call" | custom-call | flops 4731174912 | bytes 24641536 | tf_op jit(solution)/shard_map/prefix/pallas_call | solution.py:375
  26.7 0.0 collective-permute-done.3.r3
  26.8 0.0 collective-permute-done.2.r2
  26.8 0.5 collective-permute-done.1.r1
  27.3 0.3 collective-permute-start.4
  27.6 2.0 %collective-permute-done.4.refs_3_.passed = f32[3,200,256]{2,1,0:T(8,128)S(1)} collective-permute-done((f32[3,200,256]{2,1,0:T(8,128)S(1)}, f32[3,200,256]{2,1,0:T(8,128)S(1)}, u32[]{:S(2)}, u32[]{:S(2)}) %collective-permute-start.4) | collective-permute-done | bytes 614432 | tf_op jit(solution)/shard_map/ppermute | solution.py:343
  29.6 2.5 %ring_y.1 = (f32[200,256]{1,0:T(8,128)S(1)}, f32[400,256]{1,0:T(8,128)S(1)}) custom-call(s32[4]{0:T(128)S(1)} %pad_add_fusion.place.refs_0_, f32[400,256]{1,0:T(8,128)S(1)} %get-tuple-element.20.later.refs_1_, f32[3,200,256]{2,1,0:T(8,128)S(1)} %stack_y.1.refs_2_.direct, f32[3,200,256]{2,1,0:T(8,128)S(1)} %collective-permute-done.4.refs_3_.passed), custom_call_target="tpu_custom_call" | custom-call | flops 905969664 | bytes 4718592 | tf_op jit(solution)/shard_map/ring_y/pallas_call | solution.py:380
  32.1 2.8 %collective-permute-start.7 = (f32[200,256]{1,0:T(8,128)S(1)}, f32[200,256]{1,0:T(8,128)S(1)}, u32[]{:S(2)}, u32[]{:S(2)}) collective-permute-start(f32[200,256]{1,0:T(8,128)S(1)} %get-tuple-element.24), channel_id=1, source_target_pairs={{0,24},{1,25},{2,26},{3,27},{4,28},{5,29},{6,30},{7,31},{8,0},{9,1... | collective-permute-start | bytes 614408 | tf_op jit(solution)/shard_map/ppermute | solution.py:343
  34.9 0.8 collective-permute-start.6
  35.7 0.9 collective-permute-start.5
  36.6 0.7 before_y.1
  37.2 6.7 %collective-permute-done.7.r3 = f32[200,256]{1,0:T(8,128)S(1)} collective-permute-done((f32[200,256]{1,0:T(8,128)S(1)}, f32[200,256]{1,0:T(8,128)S(1)}, u32[]{:S(2)}, u32[]{:S(2)}) %collective-permute-start.7) | collective-permute-done | bytes 204832 | tf_op jit(solution)/shard_map/ppermute | solution.py:343
  44.0 0.4 collective-permute-done.6.r2
  44.4 3.2 %collective-permute-done.5.r1 = f32[200,256]{1,0:T(8,128)S(1)} collective-permute-done((f32[200,256]{1,0:T(8,128)S(1)}, f32[200,256]{1,0:T(8,128)S(1)}, u32[]{:S(2)}, u32[]{:S(2)}) %collective-permute-start.5) | collective-permute-done | bytes 204832 | tf_op jit(solution)/shard_map/ppermute | solution.py:343
  47.7 0.1 collective-permute-start.8
  47.8 2.0 %collective-permute-done.8.refs_3_.passed = f32[3,200,256]{2,1,0:T(8,128)S(1)} collective-permute-done((f32[3,200,256]{2,1,0:T(8,128)S(1)}, f32[3,200,256]{2,1,0:T(8,128)S(1)}, u32[]{:S(2)}, u32[]{:S(2)}) %collective-permute-start.8) | collective-permute-done | bytes 614432 | tf_op jit(solution)/shard_map/ppermute | solution.py:343
  49.8 3.2 %ring_x.1 = (f32[200,256]{1,0:T(8,128)S(1)}, f32[400,256]{1,0:T(8,128)}) custom-call(s32[4]{0:T(128)S(1)} %pad_add_fusion.place.refs_0_, f32[400,256]{1,0:T(8,128)S(1)} %get-tuple-element.23.later.refs_1_, f32[3,200,256]{2,1,0:T(8,128)S(1)} %stack_x.1.refs_2_.direct, f32[3,200,256]{2,1,0:T(8,128)S(1)} %collective-permute-done.8.refs_3_.passed), custom_call_target="tpu_custom_call" | custom-call | flops 905969664 | bytes 4718592 | tf_op jit(solution)/shard_map/ring_x/pallas_call | solution.py:380
  53.0 4.0 %collective-permute-start.11 = (f32[200,256]{1,0:T(8,128)S(1)}, f32[200,256]{1,0:T(8,128)S(1)}, u32[]{:S(2)}, u32[]{:S(2)}) collective-permute-start(f32[200,256]{1,0:T(8,128)S(1)} %get-tuple-element.26), channel_id=1, source_target_pairs={{0,96},{1,97},{2,98},{3,99},{4,100},{5,101},{6,102},{7,103},{8,104... | collective-permute-start | bytes 614408 | tf_op jit(solution)/shard_map/ppermute | solution.py:343
  57.0 0.0 collective-permute-start.10
  57.0 1.3 %collective-permute-start.9 = (f32[200,256]{1,0:T(8,128)S(1)}, f32[200,256]{1,0:T(8,128)S(1)}, u32[]{:S(2)}, u32[]{:S(2)}) collective-permute-start(f32[200,256]{1,0:T(8,128)S(1)} %get-tuple-element.26), channel_id=1, source_target_pairs={{0,32},{1,33},{2,34},{3,35},{4,36},{5,37},{6,38},{7,39},{8,40},{9,... | collective-permute-start | bytes 614408 | tf_op jit(solution)/shard_map/ppermute | solution.py:343
  58.3 0.0 copy-start
  58.3 0.0 copy-start.3
  58.3 0.0 copy-start.4
  58.3 1.9 %entry.1 = (f32[256,256]{1,0:T(8,128)S(1)}, f32[256,256]{1,0:T(8,128)S(1)}, f32[8,256]{1,0:T(8,128)S(1)}) custom-call(s32[4]{0:T(128)S(1)} %pad_add_fusion.place.refs_0_, f32[3,200,256]{2,1,0:T(8,128)S(1)} %stack_x.1.refs_2_.direct, f32[3,200,256]{2,1,0:T(8,128)S(1)} %collective-permute-done.8.refs_3_.passed, f32[256,256]{1,0:T(8,128)S(1)} %get-tuple-element.27.ya, ...), custom_call_target="tpu_custom_call" | custom-call | flops 1509949440 | bytes 7864320 | tf_op jit(solution)/shard_map/entry/pallas_call | solution.py:397
  60.2 5.9 %collective-permute-done.11.r3 = f32[200,256]{1,0:T(8,128)S(1)} collective-permute-done((f32[200,256]{1,0:T(8,128)S(1)}, f32[200,256]{1,0:T(8,128)S(1)}, u32[]{:S(2)}, u32[]{:S(2)}) %collective-permute-start.11) | collective-permute-done | bytes 204832 | tf_op jit(solution)/shard_map/ppermute | solution.py:343
  66.1 0.4 collective-permute-done.10.r2
  66.5 3.0 %collective-permute-done.9.r1 = f32[200,256]{1,0:T(8,128)S(1)} collective-permute-done((f32[200,256]{1,0:T(8,128)S(1)}, f32[200,256]{1,0:T(8,128)S(1)}, u32[]{:S(2)}, u32[]{:S(2)}) %collective-permute-start.9) | collective-permute-done | bytes 204832 | tf_op jit(solution)/shard_map/ppermute | solution.py:343
  69.5 0.1 collective-permute-start.12
  69.6 2.0 %collective-permute-done.12.passed = f32[3,200,256]{2,1,0:T(8,128)S(1)} collective-permute-done((f32[3,200,256]{2,1,0:T(8,128)S(1)}, f32[3,200,256]{2,1,0:T(8,128)S(1)}, u32[]{:S(2)}, u32[]{:S(2)}) %collective-permute-start.12) | collective-permute-done | bytes 614432 | tf_op jit(solution)/shard_map/ppermute | solution.py:343
  71.6 0.0 copy-done
  71.6 0.0 copy-done.3
  71.6 0.0 copy-done.4
  71.7 19.9 %final.1 = (f32[8,256]{1,0:T(8,128)}, f32[8,256,256]{2,1,0:T(8,128)}, f32[1,128]{1,0:T(1,128)S(1)}) custom-call(s32[4]{0:T(128)S(1)} %pad_add_fusion.place.refs_0_, f32[3,200,256]{2,1,0:T(8,128)S(1)} %stack_z.1.direct, f32[3,200,256]{2,1,0:T(8,128)S(1)} %collective-permute-done.12.passed, f32[256,256]{1,0:T(8,128)S(1)} %get-tuple-element.30.ea, ...), custom_call_target="tpu_custom_call" | custom-call | flops 3221225472 | bytes 16777216 | tf_op jit(solution)/shard_map/final/pallas_call | solution.py:400
  91.5 0.1 copy.8
  91.6 15.3 %all_to_all.9 = f32[128,1,1]{2,1,0:T(1,128)S(1)} all-to-all(f32[128,1,1]{2,1,0:T(1,128)S(1)} %copy.8), channel_id=1, replica_groups=mesh['z'=4,'x'=4,'y'=4,'c'=2] {'z','x','y','c'}, dimensions={0} | all-to-all | bytes 1024 | tf_op jit(solution)/shard_map/all_to_all | solution.py:416
  106.9 0.7 reduce_sum.9
  (3 shorter events, 0.1 us)
Async XLA Ops:
  0.6 0.7 copy-start.1
  1.3 14.8 %copy-start.2 = (f32[8,256]{1,0:T(8,128)S(1)}, f32[8,256]{1,0:T(8,128)}, u32[]{:S(2)}) copy-start(f32[8,256]{1,0:T(8,128)} %f_hbm.3) | copy-start | bytes 24580
  8.3 1.8 %collective-permute-start = (f32[400,256]{1,0:T(8,128)S(1)}, f32[400,256]{1,0:T(8,128)S(1)}, u32[]{:S(2)}, u32[]{:S(2)}) collective-permute-start(f32[400,256]{1,0:T(8,128)S(1)} %local.1.own), channel_id=1, source_target_pairs={{0,1},{1,0},{2,3},{3,2},{4,5},{5,4},{6,7},{7,6},{8,9},{9,8},{10,11... | collective-permute-start | bytes 1228808 | tf_op jit(solution)/shard_map/ppermute | solution.py:343
  11.4 15.4 %collective-permute-start.3 = (f32[200,256]{1,0:T(8,128)S(1)}, f32[200,256]{1,0:T(8,128)S(1)}, u32[]{:S(2)}, u32[]{:S(2)}) collective-permute-start(f32[200,256]{1,0:T(8,128)S(1)} %get-tuple-element.21), channel_id=1, source_target_pairs={{0,6},{1,7},{2,0},{3,1},{4,2},{5,3},{6,4},{7,5},{8,14},{9,15},{10,... | collective-permute-start | bytes 614408 | tf_op jit(solution)/shard_map/ppermute | solution.py:343
  14.5 12.2 %collective-permute-start.2 = (f32[200,256]{1,0:T(8,128)S(1)}, f32[200,256]{1,0:T(8,128)S(1)}, u32[]{:S(2)}, u32[]{:S(2)}) collective-permute-start(f32[200,256]{1,0:T(8,128)S(1)} %get-tuple-element.21), channel_id=1, source_target_pairs={{0,4},{1,5},{2,6},{3,7},{4,0},{5,1},{6,2},{7,3},{8,12},{9,13},{10,... | collective-permute-start | bytes 614408 | tf_op jit(solution)/shard_map/ppermute | solution.py:343
  15.2 12.1 %collective-permute-start.1 = (f32[200,256]{1,0:T(8,128)S(1)}, f32[200,256]{1,0:T(8,128)S(1)}, u32[]{:S(2)}, u32[]{:S(2)}) collective-permute-start(f32[200,256]{1,0:T(8,128)S(1)} %get-tuple-element.21), channel_id=1, source_target_pairs={{0,2},{1,3},{2,4},{3,5},{4,6},{5,7},{6,0},{7,1},{8,10},{9,11},{10,... | collective-permute-start | bytes 614408 | tf_op jit(solution)/shard_map/ppermute | solution.py:343
  27.3 2.3 %collective-permute-start.4 = (f32[3,200,256]{2,1,0:T(8,128)S(1)}, f32[3,200,256]{2,1,0:T(8,128)S(1)}, u32[]{:S(2)}, u32[]{:S(2)}) collective-permute-start(f32[3,200,256]{2,1,0:T(8,128)S(1)} %stack_y.1.refs_2_.direct), channel_id=1, source_target_pairs={{0,1},{1,0},{2,3},{3,2},{4,5},{5,4},{6,7},{7,6},{8,9},{9,8},{10,11... | collective-permute-start | bytes 1843208 | tf_op jit(solution)/shard_map/ppermute | solution.py:343
  32.1 11.9 %collective-permute-start.7 = (f32[200,256]{1,0:T(8,128)S(1)}, f32[200,256]{1,0:T(8,128)S(1)}, u32[]{:S(2)}, u32[]{:S(2)}) collective-permute-start(f32[200,256]{1,0:T(8,128)S(1)} %get-tuple-element.24), channel_id=1, source_target_pairs={{0,24},{1,25},{2,26},{3,27},{4,28},{5,29},{6,30},{7,31},{8,0},{9,1... | collective-permute-start | bytes 614408 | tf_op jit(solution)/shard_map/ppermute | solution.py:343
  34.9 9.5 %collective-permute-start.6 = (f32[200,256]{1,0:T(8,128)S(1)}, f32[200,256]{1,0:T(8,128)S(1)}, u32[]{:S(2)}, u32[]{:S(2)}) collective-permute-start(f32[200,256]{1,0:T(8,128)S(1)} %get-tuple-element.24), channel_id=1, source_target_pairs={{0,16},{1,17},{2,18},{3,19},{4,20},{5,21},{6,22},{7,23},{8,24},{9,... | collective-permute-start | bytes 614408 | tf_op jit(solution)/shard_map/ppermute | solution.py:343
  35.7 11.9 %collective-permute-start.5 = (f32[200,256]{1,0:T(8,128)S(1)}, f32[200,256]{1,0:T(8,128)S(1)}, u32[]{:S(2)}, u32[]{:S(2)}) collective-permute-start(f32[200,256]{1,0:T(8,128)S(1)} %get-tuple-element.24), channel_id=1, source_target_pairs={{0,8},{1,9},{2,10},{3,11},{4,12},{5,13},{6,14},{7,15},{8,16},{9,17... | collective-permute-start | bytes 614408 | tf_op jit(solution)/shard_map/ppermute | solution.py:343
  47.7 2.1 %collective-permute-start.8 = (f32[3,200,256]{2,1,0:T(8,128)S(1)}, f32[3,200,256]{2,1,0:T(8,128)S(1)}, u32[]{:S(2)}, u32[]{:S(2)}) collective-permute-start(f32[3,200,256]{2,1,0:T(8,128)S(1)} %stack_x.1.refs_2_.direct), channel_id=1, source_target_pairs={{0,1},{1,0},{2,3},{3,2},{4,5},{5,4},{6,7},{7,6},{8,9},{9,8},{10,11... | collective-permute-start | bytes 1843208 | tf_op jit(solution)/shard_map/ppermute | solution.py:343
  53.0 13.1 %collective-permute-start.11 = (f32[200,256]{1,0:T(8,128)S(1)}, f32[200,256]{1,0:T(8,128)S(1)}, u32[]{:S(2)}, u32[]{:S(2)}) collective-permute-start(f32[200,256]{1,0:T(8,128)S(1)} %get-tuple-element.26), channel_id=1, source_target_pairs={{0,96},{1,97},{2,98},{3,99},{4,100},{5,101},{6,102},{7,103},{8,104... | collective-permute-start | bytes 614408 | tf_op jit(solution)/shard_map/ppermute | solution.py:343
  57.0 9.5 %collective-permute-start.10 = (f32[200,256]{1,0:T(8,128)S(1)}, f32[200,256]{1,0:T(8,128)S(1)}, u32[]{:S(2)}, u32[]{:S(2)}) collective-permute-start(f32[200,256]{1,0:T(8,128)S(1)} %get-tuple-element.26), channel_id=1, source_target_pairs={{0,64},{1,65},{2,66},{3,67},{4,68},{5,69},{6,70},{7,71},{8,72},{9,... | collective-permute-start | bytes 614408 | tf_op jit(solution)/shard_map/ppermute | solution.py:343
  57.0 12.4 %collective-permute-start.9 = (f32[200,256]{1,0:T(8,128)S(1)}, f32[200,256]{1,0:T(8,128)S(1)}, u32[]{:S(2)}, u32[]{:S(2)}) collective-permute-start(f32[200,256]{1,0:T(8,128)S(1)} %get-tuple-element.26), channel_id=1, source_target_pairs={{0,32},{1,33},{2,34},{3,35},{4,36},{5,37},{6,38},{7,39},{8,40},{9,... | collective-permute-start | bytes 614408 | tf_op jit(solution)/shard_map/ppermute | solution.py:343
  58.3 13.3 %copy-start = (f32[256,256]{1,0:T(8,128)S(1)}, f32[256,256]{1,0:T(8,128)}, u32[]{:S(2)}) copy-start(f32[256,256]{1,0:T(8,128)} %l0_ref.1) | copy-start | bytes 786436
  58.3 13.3 %copy-start.3 = (f32[256]{0:T(256)S(1)}, f32[256]{0:T(256)}, u32[]{:S(2)}) copy-start(f32[256]{0:T(256)} %param.8) | copy-start | bytes 3076
  58.3 13.3 %copy-start.4 = (f32[8,256,256]{2,1,0:T(8,128)S(1)}, f32[8,256,256]{2,1,0:T(8,128)}, u32[]{:S(2)}) copy-start(f32[8,256,256]{2,1,0:T(8,128)} %get-tuple-element.32.a_ref) | copy-start | bytes 6291460
  69.5 2.1 %collective-permute-start.12 = (f32[3,200,256]{2,1,0:T(8,128)S(1)}, f32[3,200,256]{2,1,0:T(8,128)S(1)}, u32[]{:S(2)}, u32[]{:S(2)}) collective-permute-start(f32[3,200,256]{2,1,0:T(8,128)S(1)} %stack_z.1.direct), channel_id=1, source_target_pairs={{0,1},{1,0},{2,3},{3,2},{4,5},{5,4},{6,7},{7,6},{8,9},{9,8},{10,11... | collective-permute-start | bytes 1843208 | tf_op jit(solution)/shard_map/ppermute | solution.py:343
where the time goes:
time: 110 us; the launch traced here: 109 us
  Pallas kernels  47 us (43%)
  waiting for transfers between devices  27.9 us (25%)
  blocking collectives  15.3 us (14%)
  starting transfers between devices  15.1 us (14%)
  between operations  2.53 us (2%)
    ppermute x13, waiting for transfers between devices, send(): return lax.ppermute(x, AXES, ring(axis, back))  27.9 us
    pallas_call x1, Pallas kernels, on_device(): call(final_kernel, (shape(STEPS, N), stack, shape(1, H)), [SMEM] + [VMEM]...  19.9 us
    all_to_all x1, blocking collectives, on_device(): logs = lax.all_to_all(logs.reshape(H), AXES, 0, 0, tiled=True)  15.3 us
    ppermute x13, starting transfers between devices, send(): return lax.ppermute(x, AXES, ring(axis, back))  15.1 us
    pallas_call x1, Pallas kernels, on_device(): call(prefix_kernel, (stack, stack, shape(STEPS, 8, N)), steps_in + [ANY],...  10.6 us
    pallas_call x1, Pallas kernels, on_device(): call(local_kernel, (packed,), steps_in, buffers, 'local', 52, 29)  6.94 us
    pallas_call x2, Pallas kernels, ring_total(): call(lambda *refs: ring_kernel(which, *refs), (half, packed), [SMEM] + [V...  5.66 us
  transfers between devices with their start and end apart: 13, of which 11 were waited for; matrix products, arithmetic and copies ran while one was open for 0% of the time, Pallas kernels for 12%

commit v1 on v0

--- a/solution.py
+++ b/solution.py
@@ -1,3 +1,5 @@
+import functools
+
 import jax
 import jax.numpy as jnp
 from jax import lax
@@ -10,6 +12,7 @@
 N = 256
 H = 128
 STEPS = 8
+HELD = STEPS // 2
 ROWS = 400
 HALF = ROWS // 2
 PB = 8
@@ -95,18 +98,18 @@
     return z + step.cov, m + step.b
 
 
-def fetch(t_hbm, n_hbm, f_hbm, t_buf, n_buf, f_buf, sems, f_sem):
-    copies = []
+def fetch(steps, t_hbm, n_hbm, f_hbm, t_buf, n_buf, f_buf, sems, f_sem):
+    copies = {}
     pushes = pltpu.make_async_copy(f_hbm, f_buf, f_sem)
     pushes.start()
-    for k in range(STEPS):
+    for k in steps:
         pair = [
             pltpu.make_async_copy(n_hbm.at[k], n_buf.at[k], sems.at[k, 0]),
             pltpu.make_async_copy(t_hbm.at[k], t_buf.at[k], sems.at[k, 1]),
         ]
         for copy in pair:
             copy.start()
-        copies.append(pair)
+        copies[k] = pair
 
     pushes.wait()
 
@@ -121,7 +124,7 @@
 
 
 def local_kernel(t_hbm, n_hbm, f_hbm, total, *buffers):
-    one = fetch(t_hbm, n_hbm, f_hbm, *buffers)
+    one = fetch(range(STEPS), t_hbm, n_hbm, f_hbm, *buffers)
     pairs = []
     for k in range(0, STEPS, 2):
         earlier, later = one(k), one(k + 1)
@@ -130,26 +133,33 @@
     pack(total, whole.a, whole.cov, whole.b)
 
 
-def prefix_kernel(t_hbm, n_hbm, f_hbm, later, a_out, p_out, b_out, *buffers):
-    one = fetch(t_hbm, n_hbm, f_hbm, *buffers)
-
-    def put(k, step):
-        a_out[k], p_out[k], b_out[k] = step.a, step.cov, step.b
-
-    g, pairs = [], []
-    for k in range(0, STEPS, 2):
-        g += [one(k), one(k + 1)]
-        pairs.append(g[k + 1].after(g[k]))
-    put(0, g[0])
-    put(1, pairs[0])
-    put(2, g[2].after(pairs[0]))
-    front = pairs[1].after(pairs[0])
-    put(3, front)
-    put(4, g[4].after(front))
-    six = pairs[2].after(front)
-    put(5, six)
-    put(6, g[6].after(six))
-    put(7, pairs[3].after(six))
+def put_step(refs, k, step):
+    refs[0][k], refs[1][k], refs[2][k] = step.a, step.cov, step.b
+
+
+def front_kernel(t_hbm, n_hbm, f_hbm, later, a_out, p_out, b_out, *buffers):
+    out = (a_out, p_out, b_out)
+    one = fetch(range(HELD), t_hbm, n_hbm, f_hbm, *buffers)
+    first, second = one(0), one(1)
+    pair = second.after(first)
+    put_step(out, 0, first)
+    put_step(out, 1, pair)
+    third, fourth = one(2), one(3)
+    put_step(out, 2, third.after(pair))
+    put_step(out, 3, fourth.after(third).after(pair))
+
+
+def back_kernel(t_hbm, n_hbm, f_hbm, a_front, p_front, b_front, later, a_out, p_out, b_out, *buffers):
+    out = (a_out, p_out, b_out)
+    one = fetch(range(HELD, STEPS), t_hbm, n_hbm, f_hbm, *buffers)
+    fifth, sixth = one(4), one(5)
+    front = Step(a_front[HELD - 1], p_front[HELD - 1], b_front[HELD - 1])
+    put_step(out, 0, fifth.after(front))
+    six = sixth.after(fifth).after(front)
+    put_step(out, 1, six)
+    seventh, eighth = one(6), one(7)
+    put_step(out, 2, seventh.after(six))
+    put_step(out, 3, eighth.after(seventh).after(six))
 
 
 def take_half(half, whole, c):
@@ -166,7 +176,8 @@
     take_half(half, total, c)
 
 
-def stack_kernel(r1, r2, r3, beside, out):
+def stack_kernel(r1, r2, r3, *refs):
+    out = refs[-1]
     for k, r in enumerate((r1, r2, r3)):
         out[k] = r[...]
 
@@ -226,10 +237,13 @@
     return jnp.broadcast_to(x[:, i : i + 1], x.shape)
 
 
-def factor_block(rows, o):
+def factor_block(rows, o, beside):
     tiles, count = len(rows), len(rows[0])
+    share = -(-len(beside) // (count // PB))
     for q in range(0, count, PB):
         a = {(t, s): lane(rows[0][q + t], o + q + s) for t in range(PB) for s in range(t, PB)}
+        for work in beside[q // PB * share : (q // PB + 1) * share]:
+            work()
         for t in range(PB):
             inv = lax.rsqrt(a[t, t])
             u = {s: a[t, s] * inv for s in range(t + 1, PB)}
@@ -253,14 +267,33 @@
 
 def cholesky(cov, l_ref, logs_ref, u0, u1):
     us = (u0, u1)
+    r, c = grid_iota()
+    diagonals = []
+
+    def put_left(m):
+        top = u0[strided(0, H, m), :]
+        diagonals.append(jnp.sum(jnp.where(r == c, top, 0.0), axis=0, keepdims=True))
+        l_ref[m, 0:H, 0:H] = jnp.where(r <= c, top, 0.0).T
+        l_ref[m, H:, 0:H] = u1[strided(0, H, m), :].T
+        l_ref[m, 0:H, H:] = jnp.zeros((H, H), f32)
+
+    def later_rows(m, j, first, left, right):
+        cov[m, j:, H * first :] = cov[m, j:, H * first :] - mm3(left, right)
+
+    for m in range(STEPS):
+        for w in range(2):
+            us[w][strided(0, NB, m), :] = cov[m, 0:NB, H * w : H * w + H]
+    beside, outputs = [], []
     for j0 in range(0, N, NB):
         first, r0 = j0 // H, j0 + NB
         tiles = range(first, 2)
-        for m in range(STEPS):
-            for w in tiles:
-                us[w][strided(j0, NB, m), :] = cov[m, j0:r0, H * w : H * w + H]
+        if j0 == H:
+            outputs = [functools.partial(put_left, m) for m in range(STEPS)]
+        share = len(outputs) // max(1, (N - j0) // NB) if j0 >= H else 0
+        beside, outputs = beside + outputs[:share], outputs[share:]
         rows = [[us[w][pl.ds(8 * (j0 + i), 8), :] for i in range(NB)] for w in tiles]
-        factor_block(rows, j0 % H)
+        factor_block(rows, j0 % H, beside)
+        beside = []
         for w in tiles:
             for i in range(NB):
                 us[w][pl.ds(8 * (j0 + i), 8), :] = rows[w - first][i]
@@ -269,22 +302,21 @@
         for m in range(STEPS):
             u = jnp.concatenate([us[w][strided(j0, NB, m), :] for w in tiles], axis=1)
             left, right = split(u.T[r0 - H * first :, :]), split(u)
-            cov[m, r0:, H * first :] = cov[m, r0:, H * first :] - mm3(left, right)
-    r, c = grid_iota()
-    diagonals = []
+            near = cov[m, r0 : r0 + NB, H * first :] - mm3([x[:NB] for x in left], right)
+            for w in range(r0 // H, 2):
+                us[w][strided(r0, NB, m), :] = near[:, H * (w - first) : H * (w - first) + H]
+            if r0 + NB < N:
+                rest = [x[NB:] for x in left]
+                beside.append(functools.partial(later_rows, m, r0 + NB, first, rest, right))
     for m in range(STEPS):
-        a1 = u0[strided(0, H, m), :]
-        a2 = u1[strided(H, H, m), :]
-        diagonals += [jnp.sum(jnp.where(r == c, u, 0.0), axis=0, keepdims=True) for u in (a1, a2)]
-        l_ref[m, 0:H, 0:H] = jnp.where(r <= c, a1, 0.0).T
-        l_ref[m, H:, 0:H] = u1[strided(0, H, m), :].T
-        l_ref[m, H:, H:] = jnp.where(r <= c, a2, 0.0).T
-        l_ref[m, 0:H, H:] = jnp.zeros((H, H), f32)
+        low = u1[strided(H, H, m), :]
+        diagonals.append(jnp.sum(jnp.where(r == c, low, 0.0), axis=0, keepdims=True))
+        l_ref[m, H:, H:] = jnp.where(r <= c, low, 0.0).T
     logs = jnp.sum(jnp.log(jnp.concatenate(diagonals, axis=0)), axis=0, keepdims=True)
     logs_ref[...] = jnp.broadcast_to(jnp.sum(logs, axis=1, keepdims=True), (1, H))
 
 
-def final_kernel(place, direct, passed, ea, ez, eb, a_ref, p_ref, b_ref, m0_ref, l0_ref,
+def final_kernel(place, direct, passed, ea, ez, eb, a_front, p_front, b_front, a_back, p_back, b_back, m0_ref, l0_ref,
                  means, l_ref, logs, pieces, zs, ms, cov, u0, u1):
     lay_out(pieces, place, 0, direct, passed)
     l0 = split(l0_ref[...])
@@ -299,9 +331,10 @@
     z, mean = apply_to(Step(ea[...], ez[...], eb[...]), (zs[...], ms[...]))
     state = split(z + z.T)
     for k in range(STEPS):
-        spread, moved = through(split(a_ref[k]), state, mean)
-        cov[k] = spread + p_ref[k]
-        means[k : k + 1, :] = (moved + b_ref[k])[0:1, :]
+        a_ref, p_ref, b_ref = (a_front, p_front, b_front) if k < HELD else (a_back, p_back, b_back)
+        spread, moved = through(split(a_ref[k % HELD]), state, mean)
+        cov[k] = spread + p_ref[k % HELD]
+        means[k : k + 1, :] = (moved + b_ref[k % HELD])[0:1, :]
     cholesky(cov, l_ref, logs, u0, u1)
 
 
@@ -330,7 +363,7 @@
     )
 
 
-def ring(axis, back):
+def along(axis, back):
     stride, count = {"c": (1, 2), "y": (2, 4), "x": (8, 4), "z": (32, 4)}[axis]
     pairs = []
     for i in range(128):
@@ -340,13 +373,13 @@
 
 
 def send(x, axis, back):
-    return lax.ppermute(x, AXES, ring(axis, back))
-
-
-def gather_ring(half, axis, beside):
+    return lax.ppermute(x, AXES, along(axis, back))
+
+
+def gather_ring(half, axis, *beside):
     got = [send(half, axis, back) for back in (1, 2, 3)]
-    direct = call(stack_kernel, (shape(3, HALF, N),), [VMEM] * 3 + [ANY], [], "stack_" + axis, 8, 1)(
-        *got, beside
+    direct = call(stack_kernel, (shape(3, HALF, N),), [VMEM] * 3 + [ANY] * len(beside), [], "stack_" + axis, 8, 1)(
+        *got, *beside
     )[0]
     return direct, send(direct, "c", 1)
 
@@ -372,35 +405,43 @@
     mine, total = call(core_kernel, (half, packed), [SMEM, VMEM, VMEM], [], "core", 16, 3)(
         place, own, other
     )
-    a, p, b = call(
-        prefix_kernel, (stack, stack, shape(STEPS, 8, N)), steps_in + [ANY], buffers, "prefix", 52, 47
-    )(transitions, noise_factor, forcing, total)
-
-    def ring_total(which, axis, got):
-        return call(
-            lambda *refs: ring_kernel(which, *refs),
-            (half, packed),
-            [SMEM] + [VMEM] * 3,
-            lines,
-            "ring_" + axis,
-            24,
-            9,
-        )(place, total, *got)
-
-    along_y = gather_ring(mine, "y", b)
-    mine, total = ring_total(2, "y", along_y)
+    held = (shape(HELD, N, N), shape(HELD, N, N), shape(HELD, 8, N))
+    front = call(front_kernel, held, steps_in + [ANY], buffers, "front", 52, 22)(
+        transitions, noise_factor, forcing, total
+    )
+    along_y = gather_ring(mine, "y", front[2])
+    mine, total = call(
+        lambda *refs: ring_kernel(2, *refs),
+        (half, packed),
+        [SMEM] + [VMEM] * 3,
+        lines,
+        "ring_y",
+        24,
+        9,
+    )(place, total, *along_y)
     by_y = call(before_y_kernel, element, [SMEM, VMEM, VMEM, ANY], lines, "before_y", 24, 9)(
         place, *along_y, total
     )
-    along_x = gather_ring(mine, "x", by_y[2])
-    mine, total = ring_total(1, "x", along_x)
+    back = call(
+        back_kernel, held, steps_in + [VMEM] * 3 + [ANY], buffers, "back", 52, 28
+    )(transitions, noise_factor, forcing, *front, total)
+    along_x = gather_ring(mine, "x", by_y[2], back[2])
+    mine = call(
+        lambda *refs: ring_kernel(1, *refs),
+        (half,),
+        [SMEM] + [VMEM] * 3,
+        [pltpu.VMEM((ROWS, N), f32)] + lines,
+        "ring_x",
+        24,
+        9,
+    )(place, total, *along_x)[0]
     entry = call(entry_kernel, element, [SMEM] + [VMEM] * 6, lines, "entry", 24, 15)(
         place, *along_x, *by_y, other
     )
     means, factors, logs = call(
         final_kernel,
         (shape(STEPS, N), stack, shape(1, H)),
-        [SMEM] + [VMEM] * 10,
+        [SMEM] + [VMEM] * 13,
         [
             pltpu.VMEM((4, ROWS, N), f32),
             pltpu.VMEM((N, N), f32),
@@ -412,7 +453,7 @@
         "final",
         48,
         32,
-    )(place, *gather_ring(mine, "z", entry[2]), *entry, a, p, b, initial_mean[None], initial_factor)
+    )(place, *gather_ring(mine, "z", entry[2]), *entry, *front, *back, initial_mean[None], initial_factor)
     logs = lax.all_to_all(logs.reshape(H), AXES, 0, 0, tiled=True)
     log_scale = jnp.sum(logs) / (128 * STEPS * N)
     return means, factors, log_scale

time: 110 us -> 108 us (0.982)
  waiting for transfers between devices: 27.9 us -> 25.4 us
    ppermute x13, waiting for transfers between devices: 27.9 us -> 25.4 us  [send(): return lax.ppermute(x, AXES, along(axis, back))]
    pallas_call x1, Pallas kernels: 19.9 us -> 18.1 us  [on_device(): call(final_kernel, (shape(STEPS, N), stack, shape(1, H)), [SMEM] + [VMEM]...]
    pallas_call x6 -> x7, Pallas kernels: 16.4 us -> 17.9 us  [the longest x1 7.77 us: on_device(): call(back_kernel, held, steps_in + [VMEM] * 3 + [ANY], buffers, 'back', 5...]
  transfers between devices with their start and end apart: 13 -> 13, of which waited for: 11 -> 11; matrix products, arithmetic and copies ran while one was open for 0% -> 0% of each run, Pallas kernels for 12% -> 15%
where the time goes in v1:
time: 108 us; the launch traced here: 107 us
  Pallas kernels  46.9 us (43%)
  waiting for transfers between devices  25.4 us (24%)
  blocking collectives  15.2 us (14%)
  starting transfers between devices  15 us (14%)
  between operations  2.58 us (2%)
    ppermute x13, waiting for transfers between devices, send(): return lax.ppermute(x, AXES, along(axis, back))  25.4 us
    pallas_call x1, Pallas kernels, on_device(): call(final_kernel, (shape(STEPS, N), stack, shape(1, H)), [SMEM] + [VMEM]...  18.1 us
    all_to_all x1, blocking collectives, on_device(): logs = lax.all_to_all(logs.reshape(H), AXES, 0, 0, tiled=True)  15.2 us
    ppermute x13, starting transfers between devices, send(): return lax.ppermute(x, AXES, along(axis, back))  15 us
    pallas_call x1, Pallas kernels, on_device(): call(back_kernel, held, steps_in + [VMEM] * 3 + [ANY], buffers, 'back', 5...  7.77 us
    pallas_call x1, Pallas kernels, on_device(): call(local_kernel, (packed,), steps_in, buffers, 'local', 52, 29)  6.94 us
    pallas_call x1, Pallas kernels, on_device(): call(front_kernel, held, steps_in + [ANY], buffers, 'front', 52, 22)  5.08 us
    pallas_call x1, Pallas kernels, on_device(): call(lambda *refs: ring_kernel(1, *refs), (half,), [SMEM] + [VMEM] * 3, [...  2.46 us
  transfers between devices with their start and end apart: 13, of which 11 were waited for; matrix products, arithmetic and copies ran while one was open for 0% of the time, Pallas kernels for 15%

profile of v1, /device:TPU:0, one launch (start us, length us, event | category | flops | bytes accessed | tf_op | source)
XLA Modules:
  0.0 106.7 jit_solution(6601617544777851040)
XLA Ops:
  0.6 0.0 copy-start.1
  0.6 0.7 copy-done.1
  1.3 0.0 copy-start.2
  1.3 6.9 %local.1.own = f32[400,256]{1,0:T(8,128)S(1)} custom-call(f32[8,256,256]{2,1,0:T(8,128)} %t_hbm.5, f32[8,256,256]{2,1,0:T(8,128)} %n_hbm.5, f32[8,256]{1,0:T(8,128)S(1)} %copy-done.1), custom_call_target="tpu_custom_call" | custom-call | flops 2919235584 | bytes 15204352 | tf_op jit(solution)/shard_map/local/pallas_call | solution.py:401
  8.3 0.1 collective-permute-start
  8.4 0.1 pad_add_fusion.place.refs_0_
  8.5 1.6 %collective-permute-done.other.core = f32[400,256]{1,0:T(8,128)S(1)} collective-permute-done((f32[400,256]{1,0:T(8,128)S(1)}, f32[400,256]{1,0:T(8,128)S(1)}, u32[]{:S(2)}, u32[]{:S(2)}) %collective-permute-start) | collective-permute-done | bytes 409632 | tf_op jit(solution)/shard_map/ppermute | solution.py:376
  10.1 1.2 %core.1 = (f32[200,256]{1,0:T(8,128)S(1)}, f32[400,256]{1,0:T(8,128)S(1)}) custom-call(s32[4]{0:T(128)S(1)} %pad_add_fusion.place.refs_0_, f32[400,256]{1,0:T(8,128)S(1)} %local.1.own, f32[400,256]{1,0:T(8,128)S(1)} %collective-permute-done.other.core), custom_call_target="tpu_custom_call" | custom-call | flops 301989888 | bytes 1572864 | tf_op jit(solution)/shard_map/core/pallas_call | solution.py:405
  11.4 3.2 %collective-permute-start.3 = (f32[200,256]{1,0:T(8,128)S(1)}, f32[200,256]{1,0:T(8,128)S(1)}, u32[]{:S(2)}, u32[]{:S(2)}) collective-permute-start(f32[200,256]{1,0:T(8,128)S(1)} %get-tuple-element.23), channel_id=1, source_target_pairs={{0,6},{1,7},{2,0},{3,1},{4,2},{5,3},{6,4},{7,5},{8,14},{9,15},{10,... | collective-permute-start | bytes 614408 | tf_op jit(solution)/shard_map/ppermute | solution.py:376
  14.5 0.6 collective-permute-start.2
  15.2 1.0 collective-permute-start.1
  16.1 0.0 copy-done.2
  16.1 5.1 %front.1 = (f32[4,256,256]{2,1,0:T(8,128)S(1)}, f32[4,256,256]{2,1,0:T(8,128)}, f32[4,8,256]{2,1,0:T(8,128)S(1)}) custom-call(f32[8,256,256]{2,1,0:T(8,128)} %t_hbm.5, f32[8,256,256]{2,1,0:T(8,128)} %n_hbm.5, f32[8,256]{1,0:T(8,128)S(1)} %copy-done.2, f32[400,256]{1,0:T(8,128)S(1)} %get-tuple-element.22.later.refs_1_), custom_call_target="tpu_custom_call" | custom-call | flops 2214592512 | bytes 11534336 | tf_op jit(solution)/shard_map/front/pallas_call | solution.py:409
  21.2 0.0 copy-start.4
  21.2 2.3 %collective-permute-done.3.r3 = f32[200,256]{1,0:T(8,128)S(1)} collective-permute-done((f32[200,256]{1,0:T(8,128)S(1)}, f32[200,256]{1,0:T(8,128)S(1)}, u32[]{:S(2)}, u32[]{:S(2)}) %collective-permute-start.3) | collective-permute-done | bytes 204832 | tf_op jit(solution)/shard_map/ppermute | solution.py:376
  23.6 0.5 collective-permute-done.2.r2
  24.0 3.2 %collective-permute-done.1.r1 = f32[200,256]{1,0:T(8,128)S(1)} collective-permute-done((f32[200,256]{1,0:T(8,128)S(1)}, f32[200,256]{1,0:T(8,128)S(1)}, u32[]{:S(2)}, u32[]{:S(2)}) %collective-permute-start.1) | collective-permute-done | bytes 204832 | tf_op jit(solution)/shard_map/ppermute | solution.py:376
  27.3 0.1 collective-permute-start.4
  27.4 2.0 %collective-permute-done.4.refs_3_.passed = f32[3,200,256]{2,1,0:T(8,128)S(1)} collective-permute-done((f32[3,200,256]{2,1,0:T(8,128)S(1)}, f32[3,200,256]{2,1,0:T(8,128)S(1)}, u32[]{:S(2)}, u32[]{:S(2)}) %collective-permute-start.4) | collective-permute-done | bytes 614432 | tf_op jit(solution)/shard_map/ppermute | solution.py:376
  29.4 2.5 %ring_y.1 = (f32[200,256]{1,0:T(8,128)S(1)}, f32[400,256]{1,0:T(8,128)S(1)}) custom-call(s32[4]{0:T(128)S(1)} %pad_add_fusion.place.refs_0_, f32[400,256]{1,0:T(8,128)S(1)} %get-tuple-element.22.later.refs_1_, f32[3,200,256]{2,1,0:T(8,128)S(1)} %stack_y.1.refs_2_.direct, f32[3,200,256]{2,1,0:T(8,128)S(1)} %collective-permute-done.4.refs_3_.passed), custom_call_target="tpu_custom_call" | custom-call | flops 905969664 | bytes 4718592 | tf_op jit(solution)/shard_map/ring_y/pallas_call | solution.py:413
  31.9 0.0 copy-done.4
  31.9 2.8 %collective-permute-start.7 = (f32[200,256]{1,0:T(8,128)S(1)}, f32[200,256]{1,0:T(8,128)S(1)}, u32[]{:S(2)}, u32[]{:S(2)}) collective-permute-start(f32[200,256]{1,0:T(8,128)S(1)} %get-tuple-element.26), channel_id=1, source_target_pairs={{0,24},{1,25},{2,26},{3,27},{4,28},{5,29},{6,30},{7,31},{8,0},{9,1... | collective-permute-start | bytes 614408 | tf_op jit(solution)/shard_map/ppermute | solution.py:376
  34.7 0.8 collective-permute-start.6
  35.5 0.9 collective-permute-start.5
  36.4 0.8 before_y.1
  37.3 7.8 %back.1 = (f32[4,256,256]{2,1,0:T(8,128)S(1)}, f32[4,256,256]{2,1,0:T(8,128)}, f32[4,8,256]{2,1,0:T(8,128)S(1)}) custom-call(f32[8,256,256]{2,1,0:T(8,128)} %t_hbm.5, f32[8,256,256]{2,1,0:T(8,128)} %n_hbm.5, f32[8,256]{1,0:T(8,128)S(1)} %copy-done.2, f32[4,256,256]{2,1,0:T(8,128)} %copy-done.4, f32[4,256,256]{2,1,0:T(8,128)} %get-tuple-element.29.p_front, ...), custom_call_target="tpu_custom_call" | custom-call | flops 2818572288 | bytes 14680064 | tf_op jit(solution)/shard_map/back/pallas_call | solution.py:425
  45.0 0.0 collective-permute-done.7.r3
  45.0 0.0 collective-permute-done.6.r2
  45.1 2.4 %collective-permute-done.5.r1 = f32[200,256]{1,0:T(8,128)S(1)} collective-permute-done((f32[200,256]{1,0:T(8,128)S(1)}, f32[200,256]{1,0:T(8,128)S(1)}, u32[]{:S(2)}, u32[]{:S(2)}) %collective-permute-start.5) | collective-permute-done | bytes 204832 | tf_op jit(solution)/shard_map/ppermute | solution.py:376
  47.5 0.1 collective-permute-start.8
  47.6 2.0 %collective-permute-done.8.refs_3_.passed = f32[3,200,256]{2,1,0:T(8,128)S(1)} collective-permute-done((f32[3,200,256]{2,1,0:T(8,128)S(1)}, f32[3,200,256]{2,1,0:T(8,128)S(1)}, u32[]{:S(2)}, u32[]{:S(2)}) %collective-permute-start.8) | collective-permute-done | bytes 614432 | tf_op jit(solution)/shard_map/ppermute | solution.py:376
  49.6 2.5 %ring_x.1 = f32[200,256]{1,0:T(8,128)S(1)} custom-call(s32[4]{0:T(128)S(1)} %pad_add_fusion.place.refs_0_, f32[400,256]{1,0:T(8,128)S(1)} %get-tuple-element.25.later.refs_1_, f32[3,200,256]{2,1,0:T(8,128)S(1)} %stack_x.1.refs_2_.direct, f32[3,200,256]{2,1,0:T(8,128)S(1)} %collective-permute-done.8.refs_3_.passed), custom_call_target="tpu_custom_call" | custom-call | flops 905969664 | bytes 4718592 | tf_op jit(solution)/shard_map/ring_x/pallas_call | solution.py:429
  52.1 4.1 %collective-permute-start.11 = (f32[200,256]{1,0:T(8,128)S(1)}, f32[200,256]{1,0:T(8,128)S(1)}, u32[]{:S(2)}, u32[]{:S(2)}) collective-permute-start(f32[200,256]{1,0:T(8,128)S(1)} %ring_x.1), channel_id=1, source_target_pairs={{0,96},{1,97},{2,98},{3,99},{4,100},{5,101},{6,102},{7,103},{8,104... | collective-permute-start | bytes 614408 | tf_op jit(solution)/shard_map/ppermute | solution.py:376
  56.2 0.0 collective-permute-start.10
  56.2 1.3 %collective-permute-start.9 = (f32[200,256]{1,0:T(8,128)S(1)}, f32[200,256]{1,0:T(8,128)S(1)}, u32[]{:S(2)}, u32[]{:S(2)}) collective-permute-start(f32[200,256]{1,0:T(8,128)S(1)} %ring_x.1), channel_id=1, source_target_pairs={{0,32},{1,33},{2,34},{3,35},{4,36},{5,37},{6,38},{7,39},{8,40},{9,... | collective-permute-start | bytes 614408 | tf_op jit(solution)/shard_map/ppermute | solution.py:376
  57.5 0.0 copy-start
  57.5 0.0 copy-start.3
  57.5 0.0 copy-start.5
  57.5 0.0 copy-start.6
  57.5 1.9 %entry.1 = (f32[256,256]{1,0:T(8,128)S(1)}, f32[256,256]{1,0:T(8,128)S(1)}, f32[8,256]{1,0:T(8,128)S(1)}) custom-call(s32[4]{0:T(128)S(1)} %pad_add_fusion.place.refs_0_, f32[3,200,256]{2,1,0:T(8,128)S(1)} %stack_x.1.refs_2_.direct, f32[3,200,256]{2,1,0:T(8,128)S(1)} %collective-permute-done.8.refs_3_.passed, f32[256,256]{1,0:T(8,128)S(1)} %get-tuple-element.31.ya, ...), custom_call_target="tpu_custom_call" | custom-call | flops 1509949440 | bytes 7864320 | tf_op jit(solution)/shard_map/entry/pallas_call | solution.py:438
  59.4 5.9 %collective-permute-done.11.r3 = f32[200,256]{1,0:T(8,128)S(1)} collective-permute-done((f32[200,256]{1,0:T(8,128)S(1)}, f32[200,256]{1,0:T(8,128)S(1)}, u32[]{:S(2)}, u32[]{:S(2)}) %collective-permute-start.11) | collective-permute-done | bytes 204832 | tf_op jit(solution)/shard_map/ppermute | solution.py:376
  65.2 0.4 collective-permute-done.10.r2
  65.7 3.0 %collective-permute-done.9.r1 = f32[200,256]{1,0:T(8,128)S(1)} collective-permute-done((f32[200,256]{1,0:T(8,128)S(1)}, f32[200,256]{1,0:T(8,128)S(1)}, u32[]{:S(2)}, u32[]{:S(2)}) %collective-permute-start.9) | collective-permute-done | bytes 204832 | tf_op jit(solution)/shard_map/ppermute | solution.py:376
  68.7 0.1 collective-permute-start.12
  68.8 2.0 %collective-permute-done.12.passed = f32[3,200,256]{2,1,0:T(8,128)S(1)} collective-permute-done((f32[3,200,256]{2,1,0:T(8,128)S(1)}, f32[3,200,256]{2,1,0:T(8,128)S(1)}, u32[]{:S(2)}, u32[]{:S(2)}) %collective-permute-start.12) | collective-permute-done | bytes 614432 | tf_op jit(solution)/shard_map/ppermute | solution.py:376
  70.8 0.0 copy-done
  70.8 0.0 copy-done.3
  70.8 0.0 copy-done.5
  70.8 0.0 copy-done.6
  70.8 18.1 %final.1 = (f32[8,256]{1,0:T(8,128)}, f32[8,256,256]{2,1,0:T(8,128)}, f32[1,128]{1,0:T(1,128)S(1)}) custom-call(s32[4]{0:T(128)S(1)} %pad_add_fusion.place.refs_0_, f32[3,200,256]{2,1,0:T(8,128)S(1)} %stack_z.1.direct, f32[3,200,256]{2,1,0:T(8,128)S(1)} %collective-permute-done.12.passed, f32[256,256]{1,0:T(8,128)S(1)} %get-tuple-element.34.ea, ...), custom_call_target="tpu_custom_call" | custom-call | flops 3221225472 | bytes 16777216 | tf_op jit(solution)/shard_map/final/pallas_call | solution.py:441
  88.9 0.1 copy.8
  89.0 15.2 %all_to_all.9 = f32[128,1,1]{2,1,0:T(1,128)S(1)} all-to-all(f32[128,1,1]{2,1,0:T(1,128)S(1)} %copy.8), channel_id=1, replica_groups=mesh['z'=4,'x'=4,'y'=4,'c'=2] {'z','x','y','c'}, dimensions={0} | all-to-all | bytes 1024 | tf_op jit(solution)/shard_map/all_to_all | solution.py:457
  104.2 0.7 reduce_sum.9
  (3 shorter events, 0.1 us)
Async XLA Ops:
  0.6 0.7 copy-start.1
  1.3 14.8 %copy-start.2 = (f32[8,256]{1,0:T(8,128)S(1)}, f32[8,256]{1,0:T(8,128)}, u32[]{:S(2)}) copy-start(f32[8,256]{1,0:T(8,128)} %f_hbm.5) | copy-start | bytes 24580
  8.3 1.8 %collective-permute-start = (f32[400,256]{1,0:T(8,128)S(1)}, f32[400,256]{1,0:T(8,128)S(1)}, u32[]{:S(2)}, u32[]{:S(2)}) collective-permute-start(f32[400,256]{1,0:T(8,128)S(1)} %local.1.own), channel_id=1, source_target_pairs={{0,1},{1,0},{2,3},{3,2},{4,5},{5,4},{6,7},{7,6},{8,9},{9,8},{10,11... | collective-permute-start | bytes 1228808 | tf_op jit(solution)/shard_map/ppermute | solution.py:376
  11.4 12.2 %collective-permute-start.3 = (f32[200,256]{1,0:T(8,128)S(1)}, f32[200,256]{1,0:T(8,128)S(1)}, u32[]{:S(2)}, u32[]{:S(2)}) collective-permute-start(f32[200,256]{1,0:T(8,128)S(1)} %get-tuple-element.23), channel_id=1, source_target_pairs={{0,6},{1,7},{2,0},{3,1},{4,2},{5,3},{6,4},{7,5},{8,14},{9,15},{10,... | collective-permute-start | bytes 614408 | tf_op jit(solution)/shard_map/ppermute | solution.py:376
  14.5 9.5 %collective-permute-start.2 = (f32[200,256]{1,0:T(8,128)S(1)}, f32[200,256]{1,0:T(8,128)S(1)}, u32[]{:S(2)}, u32[]{:S(2)}) collective-permute-start(f32[200,256]{1,0:T(8,128)S(1)} %get-tuple-element.23), channel_id=1, source_target_pairs={{0,4},{1,5},{2,6},{3,7},{4,0},{5,1},{6,2},{7,3},{8,12},{9,13},{10,... | collective-permute-start | bytes 614408 | tf_op jit(solution)/shard_map/ppermute | solution.py:376
  15.2 12.1 %collective-permute-start.1 = (f32[200,256]{1,0:T(8,128)S(1)}, f32[200,256]{1,0:T(8,128)S(1)}, u32[]{:S(2)}, u32[]{:S(2)}) collective-permute-start(f32[200,256]{1,0:T(8,128)S(1)} %get-tuple-element.23), channel_id=1, source_target_pairs={{0,2},{1,3},{2,4},{3,5},{4,6},{5,7},{6,0},{7,1},{8,10},{9,11},{10,... | collective-permute-start | bytes 614408 | tf_op jit(solution)/shard_map/ppermute | solution.py:376
  21.2 10.7 %copy-start.4 = (f32[4,256,256]{2,1,0:T(8,128)}, f32[4,256,256]{2,1,0:T(8,128)S(1)}, u32[]{:S(2)}) copy-start(f32[4,256,256]{2,1,0:T(8,128)S(1)} %get-tuple-element.28.a_front) | copy-start | bytes 3145732
  27.3 2.1 %collective-permute-start.4 = (f32[3,200,256]{2,1,0:T(8,128)S(1)}, f32[3,200,256]{2,1,0:T(8,128)S(1)}, u32[]{:S(2)}, u32[]{:S(2)}) collective-permute-start(f32[3,200,256]{2,1,0:T(8,128)S(1)} %stack_y.1.refs_2_.direct), channel_id=1, source_target_pairs={{0,1},{1,0},{2,3},{3,2},{4,5},{5,4},{6,7},{7,6},{8,9},{9,8},{10,11... | collective-permute-start | bytes 1843208 | tf_op jit(solution)/shard_map/ppermute | solution.py:376
  31.9 13.1 %collective-permute-start.7 = (f32[200,256]{1,0:T(8,128)S(1)}, f32[200,256]{1,0:T(8,128)S(1)}, u32[]{:S(2)}, u32[]{:S(2)}) collective-permute-start(f32[200,256]{1,0:T(8,128)S(1)} %get-tuple-element.26), channel_id=1, source_target_pairs={{0,24},{1,25},{2,26},{3,27},{4,28},{5,29},{6,30},{7,31},{8,0},{9,1... | collective-permute-start | bytes 614408 | tf_op jit(solution)/shard_map/ppermute | solution.py:376
  34.7 10.3 %collective-permute-start.6 = (f32[200,256]{1,0:T(8,128)S(1)}, f32[200,256]{1,0:T(8,128)S(1)}, u32[]{:S(2)}, u32[]{:S(2)}) collective-permute-start(f32[200,256]{1,0:T(8,128)S(1)} %get-tuple-element.26), channel_id=1, source_target_pairs={{0,16},{1,17},{2,18},{3,19},{4,20},{5,21},{6,22},{7,23},{8,24},{9,... | collective-permute-start | bytes 614408 | tf_op jit(solution)/shard_map/ppermute | solution.py:376
  35.5 11.9 %collective-permute-start.5 = (f32[200,256]{1,0:T(8,128)S(1)}, f32[200,256]{1,0:T(8,128)S(1)}, u32[]{:S(2)}, u32[]{:S(2)}) collective-permute-start(f32[200,256]{1,0:T(8,128)S(1)} %get-tuple-element.26), channel_id=1, source_target_pairs={{0,8},{1,9},{2,10},{3,11},{4,12},{5,13},{6,14},{7,15},{8,16},{9,17... | collective-permute-start | bytes 614408 | tf_op jit(solution)/shard_map/ppermute | solution.py:376
  47.5 2.1 %collective-permute-start.8 = (f32[3,200,256]{2,1,0:T(8,128)S(1)}, f32[3,200,256]{2,1,0:T(8,128)S(1)}, u32[]{:S(2)}, u32[]{:S(2)}) collective-permute-start(f32[3,200,256]{2,1,0:T(8,128)S(1)} %stack_x.1.refs_2_.direct), channel_id=1, source_target_pairs={{0,1},{1,0},{2,3},{3,2},{4,5},{5,4},{6,7},{7,6},{8,9},{9,8},{10,11... | collective-permute-start | bytes 1843208 | tf_op jit(solution)/shard_map/ppermute | solution.py:376
  52.1 13.1 %collective-permute-start.11 = (f32[200,256]{1,0:T(8,128)S(1)}, f32[200,256]{1,0:T(8,128)S(1)}, u32[]{:S(2)}, u32[]{:S(2)}) collective-permute-start(f32[200,256]{1,0:T(8,128)S(1)} %ring_x.1), channel_id=1, source_target_pairs={{0,96},{1,97},{2,98},{3,99},{4,100},{5,101},{6,102},{7,103},{8,104... | collective-permute-start | bytes 614408 | tf_op jit(solution)/shard_map/ppermute | solution.py:376
  56.2 9.5 %collective-permute-start.10 = (f32[200,256]{1,0:T(8,128)S(1)}, f32[200,256]{1,0:T(8,128)S(1)}, u32[]{:S(2)}, u32[]{:S(2)}) collective-permute-start(f32[200,256]{1,0:T(8,128)S(1)} %ring_x.1), channel_id=1, source_target_pairs={{0,64},{1,65},{2,66},{3,67},{4,68},{5,69},{6,70},{7,71},{8,72},{9,... | collective-permute-start | bytes 614408 | tf_op jit(solution)/shard_map/ppermute | solution.py:376
  56.2 12.4 %collective-permute-start.9 = (f32[200,256]{1,0:T(8,128)S(1)}, f32[200,256]{1,0:T(8,128)S(1)}, u32[]{:S(2)}, u32[]{:S(2)}) collective-permute-start(f32[200,256]{1,0:T(8,128)S(1)} %ring_x.1), channel_id=1, source_target_pairs={{0,32},{1,33},{2,34},{3,35},{4,36},{5,37},{6,38},{7,39},{8,40},{9,... | collective-permute-start | bytes 614408 | tf_op jit(solution)/shard_map/ppermute | solution.py:376
  57.5 13.3 %copy-start = (f32[256,256]{1,0:T(8,128)S(1)}, f32[256,256]{1,0:T(8,128)}, u32[]{:S(2)}) copy-start(f32[256,256]{1,0:T(8,128)} %l0_ref.1) | copy-start | bytes 786436
  57.5 13.3 %copy-start.3 = (f32[256]{0:T(256)S(1)}, f32[256]{0:T(256)}, u32[]{:S(2)}) copy-start(f32[256]{0:T(256)} %param.8) | copy-start | bytes 3076
  57.5 13.4 %copy-start.5 = (f32[4,256,256]{2,1,0:T(8,128)S(1)}, f32[4,256,256]{2,1,0:T(8,128)}, u32[]{:S(2)}) copy-start(f32[4,256,256]{2,1,0:T(8,128)} %copy-done.4) | copy-start | bytes 3145732
  57.5 13.4 %copy-start.6 = (f32[4,256,256]{2,1,0:T(8,128)S(1)}, f32[4,256,256]{2,1,0:T(8,128)}, u32[]{:S(2)}) copy-start(f32[4,256,256]{2,1,0:T(8,128)} %get-tuple-element.29.p_front) | copy-start | bytes 3145732
  68.7 2.1 %collective-permute-start.12 = (f32[3,200,256]{2,1,0:T(8,128)S(1)}, f32[3,200,256]{2,1,0:T(8,128)S(1)}, u32[]{:S(2)}, u32[]{:S(2)}) collective-permute-start(f32[3,200,256]{2,1,0:T(8,128)S(1)} %stack_z.1.direct), channel_id=1, source_target_pairs={{0,1},{1,0},{2,3},{3,2},{4,5},{5,4},{6,7},{7,6},{8,9},{9,8},{10,11... | collective-permute-start | bytes 1843208 | tf_op jit(solution)/shard_map/ppermute | solution.py:376

commit v2 on v1

--- a/solution.py
+++ b/solution.py
@@ -149,17 +149,14 @@
     put_step(out, 3, fourth.after(third).after(pair))
 
 
-def back_kernel(t_hbm, n_hbm, f_hbm, a_front, p_front, b_front, later, a_out, p_out, b_out, *buffers):
+def two_kernel(k, t_hbm, n_hbm, f_hbm, a_before, p_before, b_before, later, a_out, p_out, b_out, *buffers):
     out = (a_out, p_out, b_out)
-    one = fetch(range(HELD, STEPS), t_hbm, n_hbm, f_hbm, *buffers)
-    fifth, sixth = one(4), one(5)
-    front = Step(a_front[HELD - 1], p_front[HELD - 1], b_front[HELD - 1])
-    put_step(out, 0, fifth.after(front))
-    six = sixth.after(fifth).after(front)
-    put_step(out, 1, six)
-    seventh, eighth = one(6), one(7)
-    put_step(out, 2, seventh.after(six))
-    put_step(out, 3, eighth.after(seventh).after(six))
+    one = fetch(range(k, k + 2), t_hbm, n_hbm, f_hbm, *buffers)
+    first, second = one(k), one(k + 1)
+    last = a_before.shape[0] - 1
+    before = Step(a_before[last], p_before[last], b_before[last])
+    put_step(out, 0, first.after(before))
+    put_step(out, 1, second.after(first).after(before))
 
 
 def take_half(half, whole, c):
@@ -176,20 +173,18 @@
     take_half(half, total, c)
 
 
-def stack_kernel(r1, r2, r3, *refs):
-    out = refs[-1]
-    for k, r in enumerate((r1, r2, r3)):
-        out[k] = r[...]
-
-
-def lay_out(pieces, place, which, direct, passed):
+def pass_kernel(r, *refs):
+    refs[-1][...] = r[...]
+
+
+def lay_out(pieces, place, which, halves):
     me, c = place[which], place[3]
     here = pl.multiple_of(c * HALF, 8)
     there = pl.multiple_of((1 - c) * HALF, 8)
     for back in (1, 2, 3):
         spot = lax.rem(me + 4 - back, 4)
-        pieces[spot, pl.ds(here, HALF), :] = direct[back - 1]
-        pieces[spot, pl.ds(there, HALF), :] = passed[back - 1]
+        pieces[spot, pl.ds(here, HALF), :] = halves[back - 1][...]
+        pieces[spot, pl.ds(there, HALF), :] = halves[back + 2][...]
 
 
 def neutral():
@@ -199,17 +194,17 @@
     return eye, jnp.zeros((N, N), f32), jnp.zeros((8, N), f32)
 
 
-def ring_kernel(which, place, own, direct, passed, half, total, pieces):
+def ring_kernel(which, place, own, halves, half, total, pieces):
     pieces[place[which]] = own[...]
-    lay_out(pieces, place, which, direct, passed)
+    lay_out(pieces, place, which, halves)
     g = [Step(*unpack(pieces.at[k])) for k in range(4)]
     whole = g[3].after(g[2]).after(g[1].after(g[0]))
     pack(total, whole.a, whole.cov + whole.cov.T, whole.b)
     take_half(half, total, place[3])
 
 
-def members_before(pieces, place, which, direct, passed, ea, ez, eb):
-    lay_out(pieces, place, which, direct, passed)
+def members_before(pieces, place, which, halves, ea, ez, eb):
+    lay_out(pieces, place, which, halves)
     me = place[which]
     ea[...], ez[...], eb[...] = neutral()
 
@@ -221,12 +216,14 @@
     lax.fori_loop(0, me, one, 0)
 
 
-def before_y_kernel(place, direct, passed, later, ea, ez, eb, pieces):
-    members_before(pieces, place, 2, direct, passed, ea, ez, eb)
-
-
-def entry_kernel(place, direct, passed, ya, yz, yb, core, ea, ez, eb, pieces):
-    members_before(pieces, place, 1, direct, passed, ea, ez, eb)
+def before_y_kernel(place, *refs):
+    *halves, later, ea, ez, eb, pieces = refs
+    members_before(pieces, place, 2, halves, ea, ez, eb)
+
+
+def entry_kernel(place, *refs):
+    *halves, ya, yz, yb, core, ea, ez, eb, pieces = refs
+    members_before(pieces, place, 1, halves, ea, ez, eb)
     c = place[3]
     last = Step(*[jnp.where(c == 1, u, v) for u, v in zip(unpack(core), neutral())])
     both = last.after(Step(ya[...], yz[...], yb[...])).after(Step(ea[...], ez[...], eb[...]))
@@ -316,9 +313,10 @@
     logs_ref[...] = jnp.broadcast_to(jnp.sum(logs, axis=1, keepdims=True), (1, H))
 
 
-def final_kernel(place, direct, passed, ea, ez, eb, a_front, p_front, b_front, a_back, p_back, b_back, m0_ref, l0_ref,
-                 means, l_ref, logs, pieces, zs, ms, cov, u0, u1):
-    lay_out(pieces, place, 0, direct, passed)
+def final_kernel(place, *refs):
+    *steps, m0_ref, l0_ref, means, l_ref, logs, pieces, zs, ms, cov, u0, u1 = refs[9:]
+    ea, ez, eb = refs[6:9]
+    lay_out(pieces, place, 0, refs[:6])
     l0 = split(l0_ref[...])
     zs[...] = 0.5 * mm3(l0, l0, 1, 1)
     ms[...] = jnp.broadcast_to(m0_ref[...], (8, N))
@@ -331,10 +329,11 @@
     z, mean = apply_to(Step(ea[...], ez[...], eb[...]), (zs[...], ms[...]))
     state = split(z + z.T)
     for k in range(STEPS):
-        a_ref, p_ref, b_ref = (a_front, p_front, b_front) if k < HELD else (a_back, p_back, b_back)
-        spread, moved = through(split(a_ref[k % HELD]), state, mean)
-        cov[k] = spread + p_ref[k % HELD]
-        means[k : k + 1, :] = (moved + b_ref[k % HELD])[0:1, :]
+        group, i = (0, k) if k < HELD else (3 * (1 + (k - HELD) // 2), (k - HELD) % 2)
+        a_ref, p_ref, b_ref = steps[group : group + 3]
+        spread, moved = through(split(a_ref[i]), state, mean)
+        cov[k] = spread + p_ref[i]
+        means[k : k + 1, :] = (moved + b_ref[i])[0:1, :]
     cholesky(cov, l_ref, logs, u0, u1)
 
 
@@ -378,10 +377,10 @@
 
 def gather_ring(half, axis, *beside):
     got = [send(half, axis, back) for back in (1, 2, 3)]
-    direct = call(stack_kernel, (shape(3, HALF, N),), [VMEM] * 3 + [ANY] * len(beside), [], "stack_" + axis, 8, 1)(
-        *got, *beside
+    first = call(pass_kernel, (shape(HALF, N),), [VMEM] + [ANY] * len(beside), [], "pass_" + axis, 8, 1)(
+        got[0], *beside
     )[0]
-    return direct, send(direct, "c", 1)
+    return got + [send(r, "c", 1) for r in (first, got[1], got[2])]
 
 
 def on_device(transitions, noise_factor, forcing, initial_mean, initial_factor):
@@ -409,39 +408,47 @@
     front = call(front_kernel, held, steps_in + [ANY], buffers, "front", 52, 22)(
         transitions, noise_factor, forcing, total
     )
+    two = (shape(2, N, N), shape(2, N, N), shape(2, 8, N))
+
+    def next_two(k, before, later, name):
+        return call(
+            lambda *refs: two_kernel(k, *refs), two, steps_in + [VMEM] * 3 + [ANY], buffers, name, 52, 15
+        )(transitions, noise_factor, forcing, *before, later)
+
     along_y = gather_ring(mine, "y", front[2])
     mine, total = call(
-        lambda *refs: ring_kernel(2, *refs),
+        lambda place, own, *refs: ring_kernel(2, place, own, refs[:6], *refs[6:]),
         (half, packed),
-        [SMEM] + [VMEM] * 3,
+        [SMEM] + [VMEM] * 7,
         lines,
         "ring_y",
         24,
         9,
     )(place, total, *along_y)
-    by_y = call(before_y_kernel, element, [SMEM, VMEM, VMEM, ANY], lines, "before_y", 24, 9)(
+    by_y = call(before_y_kernel, element, [SMEM] + [VMEM] * 6 + [ANY], lines, "before_y", 24, 9)(
         place, *along_y, total
     )
-    back = call(
-        back_kernel, held, steps_in + [VMEM] * 3 + [ANY], buffers, "back", 52, 28
-    )(transitions, noise_factor, forcing, *front, total)
-    along_x = gather_ring(mine, "x", by_y[2], back[2])
+    third = next_two(HELD, front, total, "third")
+    along_x = gather_ring(mine, "x", by_y[2], third[2])
     mine = call(
-        lambda *refs: ring_kernel(1, *refs),
+        lambda place, own, *refs: ring_kernel(
+            1, place, own, refs[:6], refs[6], refs[7], refs[8]
+        ),
         (half,),
-        [SMEM] + [VMEM] * 3,
+        [SMEM] + [VMEM] * 7,
         [pltpu.VMEM((ROWS, N), f32)] + lines,
         "ring_x",
         24,
         9,
     )(place, total, *along_x)[0]
-    entry = call(entry_kernel, element, [SMEM] + [VMEM] * 6, lines, "entry", 24, 15)(
+    entry = call(entry_kernel, element, [SMEM] + [VMEM] * 10, lines, "entry", 24, 15)(
         place, *along_x, *by_y, other
     )
+    fourth = next_two(HELD + 2, third, mine, "fourth")
     means, factors, logs = call(
         final_kernel,
         (shape(STEPS, N), stack, shape(1, H)),
-        [SMEM] + [VMEM] * 13,
+        [SMEM] + [VMEM] * 20,
         [
             pltpu.VMEM((4, ROWS, N), f32),
             pltpu.VMEM((N, N), f32),
@@ -453,7 +460,16 @@
         "final",
         48,
         32,
-    )(place, *gather_ring(mine, "z", entry[2]), *entry, *front, *back, initial_mean[None], initial_factor)
+    )(
+        place,
+        *gather_ring(mine, "z", entry[2], fourth[2]),
+        *entry,
+        *front,
+        *third,
+        *fourth,
+        initial_mean[None],
+        initial_factor,
+    )
     logs = lax.all_to_all(logs.reshape(H), AXES, 0, 0, tiled=True)
     log_scale = jnp.sum(logs) / (128 * STEPS * N)
     return means, factors, log_scale

time: 108 us -> 105 us (0.972)
  waiting for transfers between devices: 25.4 us -> 22.2 us
  Pallas kernels: 46.9 us -> 48 us
  blocking collectives: 15.2 us -> 14.1 us
    ppermute x13 -> x19, waiting for transfers between devices: 25.4 us -> 22.2 us  [send(): return lax.ppermute(x, AXES, along(axis, back))]
    pallas_call x8 -> x9, Pallas kernels: 15.5 us -> 16.7 us  [the longest x2 8.97 us: next_two(): call(lambda *refs: two_kernel(k, *refs), two, steps_in + [VMEM] * 3 + [AN...]
    all_to_all x1, blocking collectives: 15.2 us -> 14.1 us  [on_device(): logs = lax.all_to_all(logs.reshape(H), AXES, 0, 0, tiled=True)]
    ppermute x13 -> x19, starting transfers between devices: 15 us -> 15.2 us  [send(): return lax.ppermute(x, AXES, along(axis, back))]
  transfers between devices with their start and end apart: 13 -> 19, of which waited for: 11 -> 13; matrix products, arithmetic and copies ran while one was open for 0% -> 0% of each run, Pallas kernels for 15% -> 16%
where the time goes in v2:
time: 105 us; the launch traced here: 104 us
  Pallas kernels  48 us (46%)
  waiting for transfers between devices  22.2 us (21%)
  starting transfers between devices  15.2 us (14%)
  blocking collectives  14.1 us (13%)
  between operations  2.65 us (3%)
    ppermute x19, waiting for transfers between devices, send(): return lax.ppermute(x, AXES, along(axis, back))  22.2 us
    pallas_call x1, Pallas kernels, on_device(): call(final_kernel, (shape(STEPS, N), stack, shape(1, H)), [SMEM] + [VMEM]...  18.1 us
    ppermute x19, starting transfers between devices, send(): return lax.ppermute(x, AXES, along(axis, back))  15.2 us
    all_to_all x1, blocking collectives, on_device(): logs = lax.all_to_all(logs.reshape(H), AXES, 0, 0, tiled=True)  14.1 us
    pallas_call x2, Pallas kernels, next_two(): call(lambda *refs: two_kernel(k, *refs), two, steps_in + [VMEM] * 3 + [AN...  8.97 us
    pallas_call x1, Pallas kernels, on_device(): call(local_kernel, (packed,), steps_in, buffers, 'local', 52, 29)  6.94 us
    pallas_call x1, Pallas kernels, on_device(): call(front_kernel, held, steps_in + [ANY], buffers, 'front', 52, 22)  5.09 us
    pallas_call x1, Pallas kernels, on_device(): call(lambda place, own, *refs: ring_kernel(1, place, own, refs[:6], refs[...  2.46 us
  transfers between devices with their start and end apart: 19, of which 13 were waited for; matrix products, arithmetic and copies ran while one was open for 0% of the time, Pallas kernels for 16%

profile of v2, /device:TPU:0, one launch (start us, length us, event | category | flops | bytes accessed | tf_op | source)
XLA Modules:
  0.0 103.8 jit_solution(2993589200025033616)
XLA Ops:
  0.6 0.0 copy-start.2
  0.6 0.7 copy-done.2
  1.3 6.9 %local.1.own = f32[400,256]{1,0:T(8,128)S(1)} custom-call(f32[8,256,256]{2,1,0:T(8,128)} %refs_0_.3, f32[8,256,256]{2,1,0:T(8,128)} %refs_1_.3, f32[8,256]{1,0:T(8,128)S(1)} %copy-done.2), custom_call_target="tpu_custom_call" | custom-call | flops 2919235584 | bytes 15204352 | tf_op jit(solution)/shard_map/local/pallas_call | solution.py:400
  8.3 0.1 collective-permute-start
  8.4 0.1 pad_add_fusion.place
  8.5 1.6 %collective-permute-done.other.refs_9_ = f32[400,256]{1,0:T(8,128)S(1)} collective-permute-done((f32[400,256]{1,0:T(8,128)S(1)}, f32[400,256]{1,0:T(8,128)S(1)}, u32[]{:S(2)}, u32[]{:S(2)}) %collective-permute-start) | collective-permute-done | bytes 409632 | tf_op jit(solution)/shard_map/ppermute | solution.py:375
  10.1 1.2 %core.1 = (f32[200,256]{1,0:T(8,128)S(1)}, f32[400,256]{1,0:T(8,128)S(1)}) custom-call(s32[4]{0:T(128)S(1)} %pad_add_fusion.place, f32[400,256]{1,0:T(8,128)S(1)} %local.1.own, f32[400,256]{1,0:T(8,128)S(1)} %collective-permute-done.other.refs_9_), custom_call_target="tpu_custom_call" | custom-call | flops 301989888 | bytes 1572864 | tf_op jit(solution)/shard_map/core/pallas_call | solution.py:404
  11.4 3.2 %collective-permute-start.3 = (f32[200,256]{1,0:T(8,128)S(1)}, f32[200,256]{1,0:T(8,128)S(1)}, u32[]{:S(2)}, u32[]{:S(2)}) collective-permute-start(f32[200,256]{1,0:T(8,128)S(1)} %get-tuple-element.26), channel_id=1, source_target_pairs={{0,6},{1,7},{2,0},{3,1},{4,2},{5,3},{6,4},{7,5},{8,14},{9,15},{10,... | collective-permute-start | bytes 614408 | tf_op jit(solution)/shard_map/ppermute | solution.py:375
  14.5 0.6 collective-permute-start.2
  15.2 1.0 collective-permute-start.1
  16.1 0.0 copy-done.3
  16.1 5.1 %front.1 = (f32[4,256,256]{2,1,0:T(8,128)S(1)}, f32[4,256,256]{2,1,0:T(8,128)}, f32[4,8,256]{2,1,0:T(8,128)S(1)}) custom-call(f32[8,256,256]{2,1,0:T(8,128)} %refs_0_.3, f32[8,256,256]{2,1,0:T(8,128)} %refs_1_.3, f32[8,256]{1,0:T(8,128)S(1)} %copy-done.3, f32[400,256]{1,0:T(8,128)S(1)} %get-tuple-element.25.later.own), custom_call_target="tpu_custom_call" | custom-call | flops 2214592512 | bytes 11534336 | tf_op jit(solution)/shard_map/front/pallas_call | solution.py:408
  21.2 0.0 copy-start
  21.3 2.3 %collective-permute-done.3.refs_2_ = f32[200,256]{1,0:T(8,128)S(1)} collective-permute-done((f32[200,256]{1,0:T(8,128)S(1)}, f32[200,256]{1,0:T(8,128)S(1)}, u32[]{:S(2)}, u32[]{:S(2)}) %collective-permute-start.3) | collective-permute-done | bytes 204832 | tf_op jit(solution)/shard_map/ppermute | solution.py:375
  23.6 0.0 collective-permute-start.6
  23.6 0.5 collective-permute-done.2.refs_1_
  24.0 0.0 collective-permute-start.5
  24.1 3.2 %collective-permute-done.1.r.refs_0_ = f32[200,256]{1,0:T(8,128)S(1)} collective-permute-done((f32[200,256]{1,0:T(8,128)S(1)}, f32[200,256]{1,0:T(8,128)S(1)}, u32[]{:S(2)}, u32[]{:S(2)}) %collective-permute-start.1) | collective-permute-done | bytes 204832 | tf_op jit(solution)/shard_map/ppermute | solution.py:375
  27.3 0.1 collective-permute-start.4
  27.4 0.0 collective-permute-done.6.refs_5_
  27.4 0.0 collective-permute-done.5.refs_4_
  27.4 1.4 %collective-permute-done.4.refs_3_ = f32[200,256]{1,0:T(8,128)S(1)} collective-permute-done((f32[200,256]{1,0:T(8,128)S(1)}, f32[200,256]{1,0:T(8,128)S(1)}, u32[]{:S(2)}, u32[]{:S(2)}) %collective-permute-start.4) | collective-permute-done | bytes 204832 | tf_op jit(solution)/shard_map/ppermute | solution.py:375
  28.8 2.5 %ring_y.1 = (f32[200,256]{1,0:T(8,128)S(1)}, f32[400,256]{1,0:T(8,128)S(1)}) custom-call(s32[4]{0:T(128)S(1)} %pad_add_fusion.place, f32[400,256]{1,0:T(8,128)S(1)} %get-tuple-element.25.later.own, f32[200,256]{1,0:T(8,128)S(1)} %collective-permute-done.1.r.refs_0_, f32[200,256]{1,0:T(8,128)S(1)} %collective-permute-done.2.refs_1_, ...), custom_call_target="tpu_custom_call" | custom-call | flops 905969664 | bytes 4718592 | tf_op jit(solution)/shard_map/ring_y/pallas_call | solution.py:419
  31.3 2.8 %collective-permute-start.9 = (f32[200,256]{1,0:T(8,128)S(1)}, f32[200,256]{1,0:T(8,128)S(1)}, u32[]{:S(2)}, u32[]{:S(2)}) collective-permute-start(f32[200,256]{1,0:T(8,128)S(1)} %get-tuple-element.29), channel_id=1, source_target_pairs={{0,24},{1,25},{2,26},{3,27},{4,28},{5,29},{6,30},{7,31},{8,0},{9,1... | collective-permute-start | bytes 614408 | tf_op jit(solution)/shard_map/ppermute | solution.py:375
  34.1 0.8 collective-permute-start.8
  34.9 0.9 collective-permute-start.7
  35.8 0.8 before_y.1
  36.6 0.0 copy-done
  36.6 4.7 %third.1 = (f32[2,256,256]{2,1,0:T(8,128)S(1)}, f32[2,256,256]{2,1,0:T(8,128)S(1)}, f32[2,8,256]{2,1,0:T(8,128)S(1)}) custom-call(f32[8,256,256]{2,1,0:T(8,128)} %refs_0_.3, f32[8,256,256]{2,1,0:T(8,128)} %refs_1_.3, f32[8,256]{1,0:T(8,128)S(1)} %copy-done.3, f32[4,256,256]{2,1,0:T(8,128)} %copy-done, f32[4,256,256]{2,1,0:T(8,128)} %get-tuple-element.32.refs_4_.refs_10_, ...), custom_call_target="tpu_custom_call" | custom-call | flops 1509949440 | bytes 7864320 | tf_op jit(solution)/shard_map/third/pallas_call | solution.py:414
  41.4 0.0 copy-start.4
  41.4 1.8 %collective-permute-done.9.refs_2_ = f32[200,256]{1,0:T(8,128)S(1)} collective-permute-done((f32[200,256]{1,0:T(8,128)S(1)}, f32[200,256]{1,0:T(8,128)S(1)}, u32[]{:S(2)}, u32[]{:S(2)}) %collective-permute-start.9) | collective-permute-done | bytes 204832 | tf_op jit(solution)/shard_map/ppermute | solution.py:375
  43.2 0.0 collective-permute-start.12
  43.2 0.4 collective-permute-done.8.refs_1_
  43.6 0.1 collective-permute-start.11
  43.7 3.2 %collective-permute-done.7.r.refs_0_ = f32[200,256]{1,0:T(8,128)S(1)} collective-permute-done((f32[200,256]{1,0:T(8,128)S(1)}, f32[200,256]{1,0:T(8,128)S(1)}, u32[]{:S(2)}, u32[]{:S(2)}) %collective-permute-start.7) | collective-permute-done | bytes 204832 | tf_op jit(solution)/shard_map/ppermute | solution.py:375
  46.9 0.1 collective-permute-start.10
  47.0 0.0 collective-permute-done.12.refs_5_
  47.0 0.0 collective-permute-done.11.refs_4_
  47.0 1.4 %collective-permute-done.10.refs_3_ = f32[200,256]{1,0:T(8,128)S(1)} collective-permute-done((f32[200,256]{1,0:T(8,128)S(1)}, f32[200,256]{1,0:T(8,128)S(1)}, u32[]{:S(2)}, u32[]{:S(2)}) %collective-permute-start.10) | collective-permute-done | bytes 204832 | tf_op jit(solution)/shard_map/ppermute | solution.py:375
  48.4 2.5 %ring_x.1.refs_6_ = f32[200,256]{1,0:T(8,128)S(1)} custom-call(s32[4]{0:T(128)S(1)} %pad_add_fusion.place, f32[400,256]{1,0:T(8,128)S(1)} %get-tuple-element.28.refs_6_.own, f32[200,256]{1,0:T(8,128)S(1)} %collective-permute-done.7.r.refs_0_, f32[200,256]{1,0:T(8,128)S(1)} %collective-permute-done.8.refs_1_, f32[200,256]{1,0:T(8,128)S(1)} %collective-permute-done.9.refs_2_, ...), custom_call_target="tpu_custom_call" | custom-call | flops 905969664 | bytes 4718592 | tf_op jit(solution)/shard_map/ring_x/pallas_call | solution.py:433
  50.9 4.1 %collective-permute-start.15 = (f32[200,256]{1,0:T(8,128)S(1)}, f32[200,256]{1,0:T(8,128)S(1)}, u32[]{:S(2)}, u32[]{:S(2)}) collective-permute-start(f32[200,256]{1,0:T(8,128)S(1)} %ring_x.1.refs_6_), channel_id=1, source_target_pairs={{0,96},{1,97},{2,98},{3,99},{4,100},{5,101},{6,102},{7,103},{8,104... | collective-permute-start | bytes 614408 | tf_op jit(solution)/shard_map/ppermute | solution.py:375
  55.0 0.0 collective-permute-start.14
  55.0 1.3 %collective-permute-start.13 = (f32[200,256]{1,0:T(8,128)S(1)}, f32[200,256]{1,0:T(8,128)S(1)}, u32[]{:S(2)}, u32[]{:S(2)}) collective-permute-start(f32[200,256]{1,0:T(8,128)S(1)} %ring_x.1.refs_6_), channel_id=1, source_target_pairs={{0,32},{1,33},{2,34},{3,35},{4,36},{5,37},{6,38},{7,39},{8,40},{9,... | collective-permute-start | bytes 614408 | tf_op jit(solution)/shard_map/ppermute | solution.py:375
  56.2 0.0 copy-done.4
  56.2 4.2 %fourth.1 = (f32[2,256,256]{2,1,0:T(8,128)S(1)}, f32[2,256,256]{2,1,0:T(8,128)S(1)}, f32[2,8,256]{2,1,0:T(8,128)S(1)}) custom-call(f32[8,256,256]{2,1,0:T(8,128)} %refs_0_.3, f32[8,256,256]{2,1,0:T(8,128)} %refs_1_.3, f32[8,256]{1,0:T(8,128)S(1)} %copy-done.3, f32[2,256,256]{2,1,0:T(8,128)S(1)} %get-tuple-element.37.refs_3_.refs_12_, ...), custom_call_target="tpu_custom_call" | custom-call | flops 1509949440 | bytes 7864320 | tf_op jit(solution)/shard_map/fourth/pallas_call | solution.py:414
  60.5 0.0 copy-start.1
  60.5 0.0 copy-start.5
  60.5 0.0 copy-start.6
  60.5 0.0 copy-start.7
  60.5 1.9 %entry.1 = (f32[256,256]{1,0:T(8,128)S(1)}, f32[256,256]{1,0:T(8,128)S(1)}, f32[8,256]{1,0:T(8,128)S(1)}) custom-call(s32[4]{0:T(128)S(1)} %pad_add_fusion.place, f32[200,256]{1,0:T(8,128)S(1)} %collective-permute-done.7.r.refs_0_, f32[200,256]{1,0:T(8,128)S(1)} %collective-permute-done.8.refs_1_, f32[200,256]{1,0:T(8,128)S(1)} %collective-permute-done.9.refs_2_, ...), custom_call_target="tpu_custom_call" | custom-call | flops 1509949440 | bytes 7864320 | tf_op jit(solution)/shard_map/entry/pallas_call | solution.py:444
  62.4 1.6 %collective-permute-done.15.refs_2_ = f32[200,256]{1,0:T(8,128)S(1)} collective-permute-done((f32[200,256]{1,0:T(8,128)S(1)}, f32[200,256]{1,0:T(8,128)S(1)}, u32[]{:S(2)}, u32[]{:S(2)}) %collective-permute-start.15) | collective-permute-done | bytes 204832 | tf_op jit(solution)/shard_map/ppermute | solution.py:375
  64.0 0.0 collective-permute-start.18
  64.0 0.4 collective-permute-done.14.refs_1_
  64.4 0.1 collective-permute-start.17
  64.5 2.9 %collective-permute-done.13.r.refs_0_ = f32[200,256]{1,0:T(8,128)S(1)} collective-permute-done((f32[200,256]{1,0:T(8,128)S(1)}, f32[200,256]{1,0:T(8,128)S(1)}, u32[]{:S(2)}, u32[]{:S(2)}) %collective-permute-start.13) | collective-permute-done | bytes 204832 | tf_op jit(solution)/shard_map/ppermute | solution.py:375
  67.4 0.1 collective-permute-start.16
  67.5 0.0 collective-permute-done.18.refs_5_
  67.5 0.0 collective-permute-done.17.refs_4_
  67.5 1.4 %collective-permute-done.16.refs_3_ = f32[200,256]{1,0:T(8,128)S(1)} collective-permute-done((f32[200,256]{1,0:T(8,128)S(1)}, f32[200,256]{1,0:T(8,128)S(1)}, u32[]{:S(2)}, u32[]{:S(2)}) %collective-permute-start.16) | collective-permute-done | bytes 204832 | tf_op jit(solution)/shard_map/ppermute | solution.py:375
  69.0 0.0 copy-done.5
  69.0 18.1 %final.1 = (f32[8,256]{1,0:T(8,128)}, f32[8,256,256]{2,1,0:T(8,128)}, f32[1,128]{1,0:T(1,128)S(1)}) custom-call(s32[4]{0:T(128)S(1)} %pad_add_fusion.place, f32[200,256]{1,0:T(8,128)S(1)} %collective-permute-done.13.r.refs_0_, f32[200,256]{1,0:T(8,128)S(1)} %collective-permute-done.14.refs_1_, f32[200,256]{1,0:T(8,128)S(1)} %collective-permute-done.15.refs_2_, ...), custom_call_target="tpu_custom_call" | custom-call | flops 3221225472 | bytes 16777216 | tf_op jit(solution)/shard_map/final/pallas_call | solution.py:448
  87.1 0.1 copy.8
  87.2 14.1 %all_to_all.9 = f32[128,1,1]{2,1,0:T(1,128)S(1)} all-to-all(f32[128,1,1]{2,1,0:T(1,128)S(1)} %copy.8), channel_id=1, replica_groups=mesh['z'=4,'x'=4,'y'=4,'c'=2] {'z','x','y','c'}, dimensions={0} | all-to-all | bytes 1024 | tf_op jit(solution)/shard_map/all_to_all | solution.py:473
  101.3 0.7 reduce_sum.9
  (7 shorter events, 0.1 us)
Async XLA Ops:
  0.6 0.7 copy-start.2
  1.3 14.8 %copy-start.3 = (f32[8,256]{1,0:T(8,128)S(1)}, f32[8,256]{1,0:T(8,128)}, u32[]{:S(2)}) copy-start(f32[8,256]{1,0:T(8,128)} %refs_2_.3) | copy-start | bytes 24580
  8.3 1.8 %collective-permute-start = (f32[400,256]{1,0:T(8,128)S(1)}, f32[400,256]{1,0:T(8,128)S(1)}, u32[]{:S(2)}, u32[]{:S(2)}) collective-permute-start(f32[400,256]{1,0:T(8,128)S(1)} %local.1.own), channel_id=1, source_target_pairs={{0,1},{1,0},{2,3},{3,2},{4,5},{5,4},{6,7},{7,6},{8,9},{9,8},{10,11... | collective-permute-start | bytes 1228808 | tf_op jit(solution)/shard_map/ppermute | solution.py:375
  11.4 12.2 %collective-permute-start.3 = (f32[200,256]{1,0:T(8,128)S(1)}, f32[200,256]{1,0:T(8,128)S(1)}, u32[]{:S(2)}, u32[]{:S(2)}) collective-permute-start(f32[200,256]{1,0:T(8,128)S(1)} %get-tuple-element.26), channel_id=1, source_target_pairs={{0,6},{1,7},{2,0},{3,1},{4,2},{5,3},{6,4},{7,5},{8,14},{9,15},{10,... | collective-permute-start | bytes 614408 | tf_op jit(solution)/shard_map/ppermute | solution.py:375
  14.5 9.5 %collective-permute-start.2 = (f32[200,256]{1,0:T(8,128)S(1)}, f32[200,256]{1,0:T(8,128)S(1)}, u32[]{:S(2)}, u32[]{:S(2)}) collective-permute-start(f32[200,256]{1,0:T(8,128)S(1)} %get-tuple-element.26), channel_id=1, source_target_pairs={{0,4},{1,5},{2,6},{3,7},{4,0},{5,1},{6,2},{7,3},{8,12},{9,13},{10,... | collective-permute-start | bytes 614408 | tf_op jit(solution)/shard_map/ppermute | solution.py:375
  15.2 12.1 %collective-permute-start.1 = (f32[200,256]{1,0:T(8,128)S(1)}, f32[200,256]{1,0:T(8,128)S(1)}, u32[]{:S(2)}, u32[]{:S(2)}) collective-permute-start(f32[200,256]{1,0:T(8,128)S(1)} %get-tuple-element.26), channel_id=1, source_target_pairs={{0,2},{1,3},{2,4},{3,5},{4,6},{5,7},{6,0},{7,1},{8,10},{9,11},{10,... | collective-permute-start | bytes 614408 | tf_op jit(solution)/shard_map/ppermute | solution.py:375
  21.2 15.4 %copy-start = (f32[4,256,256]{2,1,0:T(8,128)}, f32[4,256,256]{2,1,0:T(8,128)S(1)}, u32[]{:S(2)}) copy-start(f32[4,256,256]{2,1,0:T(8,128)S(1)} %get-tuple-element.31.refs_3_.refs_9_) | copy-start | bytes 3145732
  23.6 3.8 %collective-permute-start.6 = (f32[200,256]{1,0:T(8,128)S(1)}, f32[200,256]{1,0:T(8,128)S(1)}, u32[]{:S(2)}, u32[]{:S(2)}) collective-permute-start(f32[200,256]{1,0:T(8,128)S(1)} %collective-permute-done.3.refs_2_), channel_id=1, source_target_pairs={{0,1},{1,0},{2,3},{3,2},{4,5},{5,4},{6,7},{7,6},{8,9},{9,8},{10,11... | collective-permute-start | bytes 614408 | tf_op jit(solution)/shard_map/ppermute | solution.py:375
  24.0 3.4 %collective-permute-start.5 = (f32[200,256]{1,0:T(8,128)S(1)}, f32[200,256]{1,0:T(8,128)S(1)}, u32[]{:S(2)}, u32[]{:S(2)}) collective-permute-start(f32[200,256]{1,0:T(8,128)S(1)} %collective-permute-done.2.refs_1_), channel_id=1, source_target_pairs={{0,1},{1,0},{2,3},{3,2},{4,5},{5,4},{6,7},{7,6},{8,9},{9,8},{10,11... | collective-permute-start | bytes 614408 | tf_op jit(solution)/shard_map/ppermute | solution.py:375
  27.3 1.5 %collective-permute-start.4 = (f32[200,256]{1,0:T(8,128)S(1)}, f32[200,256]{1,0:T(8,128)S(1)}, u32[]{:S(2)}, u32[]{:S(2)}) collective-permute-start(f32[200,256]{1,0:T(8,128)S(1)} %pass_y.1), channel_id=1, source_target_pairs={{0,1},{1,0},{2,3},{3,2},{4,5},{5,4},{6,7},{7,6},{8,9},{9,8},{10,11... | collective-permute-start | bytes 614408 | tf_op jit(solution)/shard_map/ppermute | solution.py:375
  31.3 11.9 %collective-permute-start.9 = (f32[200,256]{1,0:T(8,128)S(1)}, f32[200,256]{1,0:T(8,128)S(1)}, u32[]{:S(2)}, u32[]{:S(2)}) collective-permute-start(f32[200,256]{1,0:T(8,128)S(1)} %get-tuple-element.29), channel_id=1, source_target_pairs={{0,24},{1,25},{2,26},{3,27},{4,28},{5,29},{6,30},{7,31},{8,0},{9,1... | collective-permute-start | bytes 614408 | tf_op jit(solution)/shard_map/ppermute | solution.py:375
  34.1 9.5 %collective-permute-start.8 = (f32[200,256]{1,0:T(8,128)S(1)}, f32[200,256]{1,0:T(8,128)S(1)}, u32[]{:S(2)}, u32[]{:S(2)}) collective-permute-start(f32[200,256]{1,0:T(8,128)S(1)} %get-tuple-element.29), channel_id=1, source_target_pairs={{0,16},{1,17},{2,18},{3,19},{4,20},{5,21},{6,22},{7,23},{8,24},{9,... | collective-permute-start | bytes 614408 | tf_op jit(solution)/shard_map/ppermute | solution.py:375
  34.9 11.9 %collective-permute-start.7 = (f32[200,256]{1,0:T(8,128)S(1)}, f32[200,256]{1,0:T(8,128)S(1)}, u32[]{:S(2)}, u32[]{:S(2)}) collective-permute-start(f32[200,256]{1,0:T(8,128)S(1)} %get-tuple-element.29), channel_id=1, source_target_pairs={{0,8},{1,9},{2,10},{3,11},{4,12},{5,13},{6,14},{7,15},{8,16},{9,17... | collective-permute-start | bytes 614408 | tf_op jit(solution)/shard_map/ppermute | solution.py:375
  41.4 14.8 %copy-start.4 = (f32[2,256,256]{2,1,0:T(8,128)}, f32[2,256,256]{2,1,0:T(8,128)S(1)}, u32[]{:S(2)}) copy-start(f32[2,256,256]{2,1,0:T(8,128)S(1)} %get-tuple-element.38.refs_4_.refs_13_) | copy-start | bytes 1572868
  43.2 3.8 %collective-permute-start.12 = (f32[200,256]{1,0:T(8,128)S(1)}, f32[200,256]{1,0:T(8,128)S(1)}, u32[]{:S(2)}, u32[]{:S(2)}) collective-permute-start(f32[200,256]{1,0:T(8,128)S(1)} %collective-permute-done.9.refs_2_), channel_id=1, source_target_pairs={{0,1},{1,0},{2,3},{3,2},{4,5},{5,4},{6,7},{7,6},{8,9},{9,8},{10,11... | collective-permute-start | bytes 614408 | tf_op jit(solution)/shard_map/ppermute | solution.py:375
  43.6 3.4 %collective-permute-start.11 = (f32[200,256]{1,0:T(8,128)S(1)}, f32[200,256]{1,0:T(8,128)S(1)}, u32[]{:S(2)}, u32[]{:S(2)}) collective-permute-start(f32[200,256]{1,0:T(8,128)S(1)} %collective-permute-done.8.refs_1_), channel_id=1, source_target_pairs={{0,1},{1,0},{2,3},{3,2},{4,5},{5,4},{6,7},{7,6},{8,9},{9,8},{10,11... | collective-permute-start | bytes 614408 | tf_op jit(solution)/shard_map/ppermute | solution.py:375
  46.9 1.5 %collective-permute-start.10 = (f32[200,256]{1,0:T(8,128)S(1)}, f32[200,256]{1,0:T(8,128)S(1)}, u32[]{:S(2)}, u32[]{:S(2)}) collective-permute-start(f32[200,256]{1,0:T(8,128)S(1)} %pass_x.1), channel_id=1, source_target_pairs={{0,1},{1,0},{2,3},{3,2},{4,5},{5,4},{6,7},{7,6},{8,9},{9,8},{10,11... | collective-permute-start | bytes 614408 | tf_op jit(solution)/shard_map/ppermute | solution.py:375
  50.9 13.1 %collective-permute-start.15 = (f32[200,256]{1,0:T(8,128)S(1)}, f32[200,256]{1,0:T(8,128)S(1)}, u32[]{:S(2)}, u32[]{:S(2)}) collective-permute-start(f32[200,256]{1,0:T(8,128)S(1)} %ring_x.1.refs_6_), channel_id=1, source_target_pairs={{0,96},{1,97},{2,98},{3,99},{4,100},{5,101},{6,102},{7,103},{8,104... | collective-permute-start | bytes 614408 | tf_op jit(solution)/shard_map/ppermute | solution.py:375
  55.0 9.5 %collective-permute-start.14 = (f32[200,256]{1,0:T(8,128)S(1)}, f32[200,256]{1,0:T(8,128)S(1)}, u32[]{:S(2)}, u32[]{:S(2)}) collective-permute-start(f32[200,256]{1,0:T(8,128)S(1)} %ring_x.1.refs_6_), channel_id=1, source_target_pairs={{0,64},{1,65},{2,66},{3,67},{4,68},{5,69},{6,70},{7,71},{8,72},{9,... | collective-permute-start | bytes 614408 | tf_op jit(solution)/shard_map/ppermute | solution.py:375
  55.0 12.4 %collective-permute-start.13 = (f32[200,256]{1,0:T(8,128)S(1)}, f32[200,256]{1,0:T(8,128)S(1)}, u32[]{:S(2)}, u32[]{:S(2)}) collective-permute-start(f32[200,256]{1,0:T(8,128)S(1)} %ring_x.1.refs_6_), channel_id=1, source_target_pairs={{0,32},{1,33},{2,34},{3,35},{4,36},{5,37},{6,38},{7,39},{8,40},{9,... | collective-permute-start | bytes 614408 | tf_op jit(solution)/shard_map/ppermute | solution.py:375
  60.5 8.5 %copy-start.1 = (f32[4,256,256]{2,1,0:T(8,128)S(1)}, f32[4,256,256]{2,1,0:T(8,128)}, u32[]{:S(2)}) copy-start(f32[4,256,256]{2,1,0:T(8,128)} %copy-done) | copy-start | bytes 3145732
  60.5 8.5 %copy-start.5 = (f32[2,256,256]{2,1,0:T(8,128)S(1)}, f32[2,256,256]{2,1,0:T(8,128)}, u32[]{:S(2)}) copy-start(f32[2,256,256]{2,1,0:T(8,128)} %copy-done.4) | copy-start | bytes 1572868
  60.5 8.5 %copy-start.6 = (f32[256,256]{1,0:T(8,128)S(1)}, f32[256,256]{1,0:T(8,128)}, u32[]{:S(2)}) copy-start(f32[256,256]{1,0:T(8,128)} %refs_19_.1) | copy-start | bytes 786436
  60.5 8.5 %copy-start.7 = (f32[256]{0:T(256)S(1)}, f32[256]{0:T(256)}, u32[]{:S(2)}) copy-start(f32[256]{0:T(256)} %param.8) | copy-start | bytes 3076
  64.0 3.5 %collective-permute-start.18 = (f32[200,256]{1,0:T(8,128)S(1)}, f32[200,256]{1,0:T(8,128)S(1)}, u32[]{:S(2)}, u32[]{:S(2)}) collective-permute-start(f32[200,256]{1,0:T(8,128)S(1)} %collective-permute-done.15.refs_2_), channel_id=1, source_target_pairs={{0,1},{1,0},{2,3},{3,2},{4,5},{5,4},{6,7},{7,6},{8,9},{9,8},{10,11... | collective-permute-start | bytes 614408 | tf_op jit(solution)/shard_map/ppermute | solution.py:375
  64.4 3.1 %collective-permute-start.17 = (f32[200,256]{1,0:T(8,128)S(1)}, f32[200,256]{1,0:T(8,128)S(1)}, u32[]{:S(2)}, u32[]{:S(2)}) collective-permute-start(f32[200,256]{1,0:T(8,128)S(1)} %collective-permute-done.14.refs_1_), channel_id=1, source_target_pairs={{0,1},{1,0},{2,3},{3,2},{4,5},{5,4},{6,7},{7,6},{8,9},{9,8},{10,11... | collective-permute-start | bytes 614408 | tf_op jit(solution)/shard_map/ppermute | solution.py:375
  67.4 1.5 %collective-permute-start.16 = (f32[200,256]{1,0:T(8,128)S(1)}, f32[200,256]{1,0:T(8,128)S(1)}, u32[]{:S(2)}, u32[]{:S(2)}) collective-permute-start(f32[200,256]{1,0:T(8,128)S(1)} %pass_z.1), channel_id=1, source_target_pairs={{0,1},{1,0},{2,3},{3,2},{4,5},{5,4},{6,7},{7,6},{8,9},{9,8},{10,11... | collective-permute-start | bytes 614408 | tf_op jit(solution)/shard_map/ppermute | solution.py:375

commit v3 on v2

--- a/solution.py
+++ b/solution.py
@@ -458,7 +458,7 @@
             pltpu.VMEM((STEPS * N, H), f32),
         ],
         "final",
-        48,
+        40,
         32,
     )(
         place,

time: 105 us -> 104 us (level)
  no operation moved by 1% of the time
where the time goes in v3:
time: 104 us; the launch traced here: 103 us
  Pallas kernels  47.4 us (46%)
  waiting for transfers between devices  22.2 us (21%)
  starting transfers between devices  15.2 us (15%)
  blocking collectives  14.1 us (14%)
  between operations  2.66 us (3%)
    ppermute x19, waiting for transfers between devices, send(): return lax.ppermute(x, AXES, along(axis, back))  22.2 us
    pallas_call x1, Pallas kernels, on_device(): call(final_kernel, (shape(STEPS, N), stack, shape(1, H)), [SMEM] + [VMEM]...  17.4 us
    ppermute x19, starting transfers between devices, send(): return lax.ppermute(x, AXES, along(axis, back))  15.2 us
    all_to_all x1, blocking collectives, on_device(): logs = lax.all_to_all(logs.reshape(H), AXES, 0, 0, tiled=True)  14.1 us
    pallas_call x2, Pallas kernels, next_two(): call(lambda *refs: two_kernel(k, *refs), two, steps_in + [VMEM] * 3 + [AN...  8.97 us
    pallas_call x1, Pallas kernels, on_device(): call(local_kernel, (packed,), steps_in, buffers, 'local', 52, 29)  6.94 us
    pallas_call x1, Pallas kernels, on_device(): call(front_kernel, held, steps_in + [ANY], buffers, 'front', 52, 22)  5.08 us
    pallas_call x1, Pallas kernels, on_device(): call(lambda place, own, *refs: ring_kernel(1, place, own, refs[:6], refs[...  2.46 us
  transfers between devices with their start and end apart: 19, of which 13 were waited for; matrix products, arithmetic and copies ran while one was open for 0% of the time, Pallas kernels for 16%

profile of v3, /device:TPU:0, one launch (start us, length us, event | category | flops | bytes accessed | tf_op | source)
XLA Modules:
  0.0 103.2 jit_solution(16662776928929915816)
XLA Ops:
  0.6 0.0 copy-start.3
  0.6 0.7 copy-done.3
  1.3 6.9 %local.1.own = f32[400,256]{1,0:T(8,128)S(1)} custom-call(f32[8,256,256]{2,1,0:T(8,128)} %refs_0_.3, f32[8,256,256]{2,1,0:T(8,128)} %refs_1_.3, f32[8,256]{1,0:T(8,128)S(1)} %copy-done.3), custom_call_target="tpu_custom_call" | custom-call | flops 2919235584 | bytes 15204352 | tf_op jit(solution)/shard_map/local/pallas_call | solution.py:400
  8.3 0.1 collective-permute-start
  8.4 0.1 pad_add_fusion.place
  8.5 1.6 %collective-permute-done.other.refs_9_ = f32[400,256]{1,0:T(8,128)S(1)} collective-permute-done((f32[400,256]{1,0:T(8,128)S(1)}, f32[400,256]{1,0:T(8,128)S(1)}, u32[]{:S(2)}, u32[]{:S(2)}) %collective-permute-start) | collective-permute-done | bytes 409632 | tf_op jit(solution)/shard_map/ppermute | solution.py:375
  10.1 1.2 %core.1 = (f32[200,256]{1,0:T(8,128)S(1)}, f32[400,256]{1,0:T(8,128)S(1)}) custom-call(s32[4]{0:T(128)S(1)} %pad_add_fusion.place, f32[400,256]{1,0:T(8,128)S(1)} %local.1.own, f32[400,256]{1,0:T(8,128)S(1)} %collective-permute-done.other.refs_9_), custom_call_target="tpu_custom_call" | custom-call | flops 301989888 | bytes 1572864 | tf_op jit(solution)/shard_map/core/pallas_call | solution.py:404
  11.4 3.2 %collective-permute-start.3 = (f32[200,256]{1,0:T(8,128)S(1)}, f32[200,256]{1,0:T(8,128)S(1)}, u32[]{:S(2)}, u32[]{:S(2)}) collective-permute-start(f32[200,256]{1,0:T(8,128)S(1)} %get-tuple-element.26), channel_id=1, source_target_pairs={{0,6},{1,7},{2,0},{3,1},{4,2},{5,3},{6,4},{7,5},{8,14},{9,15},{10,... | collective-permute-start | bytes 614408 | tf_op jit(solution)/shard_map/ppermute | solution.py:375
  14.5 0.6 collective-permute-start.2
  15.2 1.0 collective-permute-start.1
  16.1 0.0 copy-done.4
  16.1 5.1 %front.1 = (f32[4,256,256]{2,1,0:T(8,128)S(1)}, f32[4,256,256]{2,1,0:T(8,128)}, f32[4,8,256]{2,1,0:T(8,128)S(1)}) custom-call(f32[8,256,256]{2,1,0:T(8,128)} %refs_0_.3, f32[8,256,256]{2,1,0:T(8,128)} %refs_1_.3, f32[8,256]{1,0:T(8,128)S(1)} %copy-done.4, f32[400,256]{1,0:T(8,128)S(1)} %get-tuple-element.25.later.own), custom_call_target="tpu_custom_call" | custom-call | flops 2214592512 | bytes 11534336 | tf_op jit(solution)/shard_map/front/pallas_call | solution.py:408
  21.2 0.0 copy-start
  21.2 2.3 %collective-permute-done.3.refs_2_ = f32[200,256]{1,0:T(8,128)S(1)} collective-permute-done((f32[200,256]{1,0:T(8,128)S(1)}, f32[200,256]{1,0:T(8,128)S(1)}, u32[]{:S(2)}, u32[]{:S(2)}) %collective-permute-start.3) | collective-permute-done | bytes 204832 | tf_op jit(solution)/shard_map/ppermute | solution.py:375
  23.6 0.0 collective-permute-start.6
  23.6 0.5 collective-permute-done.2.refs_1_
  24.0 0.0 collective-permute-start.5
  24.1 3.2 %collective-permute-done.1.r.refs_0_ = f32[200,256]{1,0:T(8,128)S(1)} collective-permute-done((f32[200,256]{1,0:T(8,128)S(1)}, f32[200,256]{1,0:T(8,128)S(1)}, u32[]{:S(2)}, u32[]{:S(2)}) %collective-permute-start.1) | collective-permute-done | bytes 204832 | tf_op jit(solution)/shard_map/ppermute | solution.py:375
  27.3 0.1 collective-permute-start.4
  27.4 0.0 collective-permute-done.6.refs_5_
  27.4 0.0 collective-permute-done.5.refs_4_
  27.4 1.4 %collective-permute-done.4.refs_3_ = f32[200,256]{1,0:T(8,128)S(1)} collective-permute-done((f32[200,256]{1,0:T(8,128)S(1)}, f32[200,256]{1,0:T(8,128)S(1)}, u32[]{:S(2)}, u32[]{:S(2)}) %collective-permute-start.4) | collective-permute-done | bytes 204832 | tf_op jit(solution)/shard_map/ppermute | solution.py:375
  28.8 2.5 %ring_y.1 = (f32[200,256]{1,0:T(8,128)S(1)}, f32[400,256]{1,0:T(8,128)S(1)}) custom-call(s32[4]{0:T(128)S(1)} %pad_add_fusion.place, f32[400,256]{1,0:T(8,128)S(1)} %get-tuple-element.25.later.own, f32[200,256]{1,0:T(8,128)S(1)} %collective-permute-done.1.r.refs_0_, f32[200,256]{1,0:T(8,128)S(1)} %collective-permute-done.2.refs_1_, ...), custom_call_target="tpu_custom_call" | custom-call | flops 905969664 | bytes 4718592 | tf_op jit(solution)/shard_map/ring_y/pallas_call | solution.py:419
  31.3 2.8 %collective-permute-start.9 = (f32[200,256]{1,0:T(8,128)S(1)}, f32[200,256]{1,0:T(8,128)S(1)}, u32[]{:S(2)}, u32[]{:S(2)}) collective-permute-start(f32[200,256]{1,0:T(8,128)S(1)} %get-tuple-element.29), channel_id=1, source_target_pairs={{0,24},{1,25},{2,26},{3,27},{4,28},{5,29},{6,30},{7,31},{8,0},{9,1... | collective-permute-start | bytes 614408 | tf_op jit(solution)/shard_map/ppermute | solution.py:375
  34.1 0.8 collective-permute-start.8
  34.9 0.9 collective-permute-start.7
  35.8 0.8 before_y.1
  36.6 0.0 copy-done
  36.6 4.7 %third.1 = (f32[2,256,256]{2,1,0:T(8,128)S(1)}, f32[2,256,256]{2,1,0:T(8,128)S(1)}, f32[2,8,256]{2,1,0:T(8,128)S(1)}) custom-call(f32[8,256,256]{2,1,0:T(8,128)} %refs_0_.3, f32[8,256,256]{2,1,0:T(8,128)} %refs_1_.3, f32[8,256]{1,0:T(8,128)S(1)} %copy-done.4, f32[4,256,256]{2,1,0:T(8,128)} %copy-done, f32[4,256,256]{2,1,0:T(8,128)} %get-tuple-element.32.refs_4_.refs_10_, ...), custom_call_target="tpu_custom_call" | custom-call | flops 1509949440 | bytes 7864320 | tf_op jit(solution)/shard_map/third/pallas_call | solution.py:414
  41.4 0.0 copy-start.5
  41.4 1.8 %collective-permute-done.9.refs_2_ = f32[200,256]{1,0:T(8,128)S(1)} collective-permute-done((f32[200,256]{1,0:T(8,128)S(1)}, f32[200,256]{1,0:T(8,128)S(1)}, u32[]{:S(2)}, u32[]{:S(2)}) %collective-permute-start.9) | collective-permute-done | bytes 204832 | tf_op jit(solution)/shard_map/ppermute | solution.py:375
  43.2 0.0 collective-permute-start.12
  43.2 0.4 collective-permute-done.8.refs_1_
  43.6 0.1 collective-permute-start.11
  43.7 3.2 %collective-permute-done.7.r.refs_0_ = f32[200,256]{1,0:T(8,128)S(1)} collective-permute-done((f32[200,256]{1,0:T(8,128)S(1)}, f32[200,256]{1,0:T(8,128)S(1)}, u32[]{:S(2)}, u32[]{:S(2)}) %collective-permute-start.7) | collective-permute-done | bytes 204832 | tf_op jit(solution)/shard_map/ppermute | solution.py:375
  46.9 0.1 collective-permute-start.10
  47.0 0.0 collective-permute-done.12.refs_5_
  47.0 0.0 collective-permute-done.11.refs_4_
  47.0 1.4 %collective-permute-done.10.refs_3_ = f32[200,256]{1,0:T(8,128)S(1)} collective-permute-done((f32[200,256]{1,0:T(8,128)S(1)}, f32[200,256]{1,0:T(8,128)S(1)}, u32[]{:S(2)}, u32[]{:S(2)}) %collective-permute-start.10) | collective-permute-done | bytes 204832 | tf_op jit(solution)/shard_map/ppermute | solution.py:375
  48.4 2.5 %ring_x.1.refs_6_ = f32[200,256]{1,0:T(8,128)S(1)} custom-call(s32[4]{0:T(128)S(1)} %pad_add_fusion.place, f32[400,256]{1,0:T(8,128)S(1)} %get-tuple-element.28.refs_6_.own, f32[200,256]{1,0:T(8,128)S(1)} %collective-permute-done.7.r.refs_0_, f32[200,256]{1,0:T(8,128)S(1)} %collective-permute-done.8.refs_1_, f32[200,256]{1,0:T(8,128)S(1)} %collective-permute-done.9.refs_2_, ...), custom_call_target="tpu_custom_call" | custom-call | flops 905969664 | bytes 4718592 | tf_op jit(solution)/shard_map/ring_x/pallas_call | solution.py:433
  50.9 4.1 %collective-permute-start.15 = (f32[200,256]{1,0:T(8,128)S(1)}, f32[200,256]{1,0:T(8,128)S(1)}, u32[]{:S(2)}, u32[]{:S(2)}) collective-permute-start(f32[200,256]{1,0:T(8,128)S(1)} %ring_x.1.refs_6_), channel_id=1, source_target_pairs={{0,96},{1,97},{2,98},{3,99},{4,100},{5,101},{6,102},{7,103},{8,104... | collective-permute-start | bytes 614408 | tf_op jit(solution)/shard_map/ppermute | solution.py:375
  55.0 0.0 collective-permute-start.14
  55.0 1.3 %collective-permute-start.13 = (f32[200,256]{1,0:T(8,128)S(1)}, f32[200,256]{1,0:T(8,128)S(1)}, u32[]{:S(2)}, u32[]{:S(2)}) collective-permute-start(f32[200,256]{1,0:T(8,128)S(1)} %ring_x.1.refs_6_), channel_id=1, source_target_pairs={{0,32},{1,33},{2,34},{3,35},{4,36},{5,37},{6,38},{7,39},{8,40},{9,... | collective-permute-start | bytes 614408 | tf_op jit(solution)/shard_map/ppermute | solution.py:375
  56.2 0.0 copy-done.5
  56.2 4.2 %fourth.1 = (f32[2,256,256]{2,1,0:T(8,128)S(1)}, f32[2,256,256]{2,1,0:T(8,128)S(1)}, f32[2,8,256]{2,1,0:T(8,128)S(1)}) custom-call(f32[8,256,256]{2,1,0:T(8,128)} %refs_0_.3, f32[8,256,256]{2,1,0:T(8,128)} %refs_1_.3, f32[8,256]{1,0:T(8,128)S(1)} %copy-done.4, f32[2,256,256]{2,1,0:T(8,128)S(1)} %get-tuple-element.37.refs_3_.refs_12_, ...), custom_call_target="tpu_custom_call" | custom-call | flops 1509949440 | bytes 7864320 | tf_op jit(solution)/shard_map/fourth/pallas_call | solution.py:414
  60.5 0.0 copy-start.1
  60.5 0.0 copy-start.2
  60.5 0.0 copy-start.7
  60.5 0.0 copy-start.8
  60.5 1.9 %entry.1 = (f32[256,256]{1,0:T(8,128)S(1)}, f32[256,256]{1,0:T(8,128)S(1)}, f32[8,256]{1,0:T(8,128)S(1)}) custom-call(s32[4]{0:T(128)S(1)} %pad_add_fusion.place, f32[200,256]{1,0:T(8,128)S(1)} %collective-permute-done.7.r.refs_0_, f32[200,256]{1,0:T(8,128)S(1)} %collective-permute-done.8.refs_1_, f32[200,256]{1,0:T(8,128)S(1)} %collective-permute-done.9.refs_2_, ...), custom_call_target="tpu_custom_call" | custom-call | flops 1509949440 | bytes 7864320 | tf_op jit(solution)/shard_map/entry/pallas_call | solution.py:444
  62.4 1.6 %collective-permute-done.15.refs_2_ = f32[200,256]{1,0:T(8,128)S(1)} collective-permute-done((f32[200,256]{1,0:T(8,128)S(1)}, f32[200,256]{1,0:T(8,128)S(1)}, u32[]{:S(2)}, u32[]{:S(2)}) %collective-permute-start.15) | collective-permute-done | bytes 204832 | tf_op jit(solution)/shard_map/ppermute | solution.py:375
  64.0 0.0 collective-permute-start.18
  64.0 0.4 collective-permute-done.14.refs_1_
  64.4 0.1 collective-permute-start.17
  64.5 2.9 %collective-permute-done.13.r.refs_0_ = f32[200,256]{1,0:T(8,128)S(1)} collective-permute-done((f32[200,256]{1,0:T(8,128)S(1)}, f32[200,256]{1,0:T(8,128)S(1)}, u32[]{:S(2)}, u32[]{:S(2)}) %collective-permute-start.13) | collective-permute-done | bytes 204832 | tf_op jit(solution)/shard_map/ppermute | solution.py:375
  67.4 0.1 collective-permute-start.16
  67.5 0.0 collective-permute-done.18.refs_5_
  67.5 0.0 collective-permute-done.17.refs_4_
  67.5 1.4 %collective-permute-done.16.refs_3_ = f32[200,256]{1,0:T(8,128)S(1)} collective-permute-done((f32[200,256]{1,0:T(8,128)S(1)}, f32[200,256]{1,0:T(8,128)S(1)}, u32[]{:S(2)}, u32[]{:S(2)}) %collective-permute-start.16) | collective-permute-done | bytes 204832 | tf_op jit(solution)/shard_map/ppermute | solution.py:375
  69.0 0.0 copy-done.2
  69.0 17.4 %final.1 = (f32[8,256]{1,0:T(8,128)}, f32[8,256,256]{2,1,0:T(8,128)}, f32[1,128]{1,0:T(1,128)S(1)}) custom-call(s32[4]{0:T(128)S(1)} %pad_add_fusion.place, f32[200,256]{1,0:T(8,128)S(1)} %collective-permute-done.13.r.refs_0_, f32[200,256]{1,0:T(8,128)S(1)} %collective-permute-done.14.refs_1_, f32[200,256]{1,0:T(8,128)S(1)} %collective-permute-done.15.refs_2_, ...), custom_call_target="tpu_custom_call" | custom-call | flops 3221225472 | bytes 16777216 | tf_op jit(solution)/shard_map/final/pallas_call | solution.py:448
  86.4 0.1 copy.8
  86.5 14.1 %all_to_all.9 = f32[128,1,1]{2,1,0:T(1,128)S(1)} all-to-all(f32[128,1,1]{2,1,0:T(1,128)S(1)} %copy.8), channel_id=1, replica_groups=mesh['z'=4,'x'=4,'y'=4,'c'=2] {'z','x','y','c'}, dimensions={0} | all-to-all | bytes 1024 | tf_op jit(solution)/shard_map/all_to_all | solution.py:473
  100.7 0.7 reduce_sum.9
  (9 shorter events, 0.1 us)
Async XLA Ops:
  0.6 0.7 copy-start.3
  1.3 14.8 %copy-start.4 = (f32[8,256]{1,0:T(8,128)S(1)}, f32[8,256]{1,0:T(8,128)}, u32[]{:S(2)}) copy-start(f32[8,256]{1,0:T(8,128)} %refs_2_.3) | copy-start | bytes 24580
  8.3 1.8 %collective-permute-start = (f32[400,256]{1,0:T(8,128)S(1)}, f32[400,256]{1,0:T(8,128)S(1)}, u32[]{:S(2)}, u32[]{:S(2)}) collective-permute-start(f32[400,256]{1,0:T(8,128)S(1)} %local.1.own), channel_id=1, source_target_pairs={{0,1},{1,0},{2,3},{3,2},{4,5},{5,4},{6,7},{7,6},{8,9},{9,8},{10,11... | collective-permute-start | bytes 1228808 | tf_op jit(solution)/shard_map/ppermute | solution.py:375
  11.4 12.2 %collective-permute-start.3 = (f32[200,256]{1,0:T(8,128)S(1)}, f32[200,256]{1,0:T(8,128)S(1)}, u32[]{:S(2)}, u32[]{:S(2)}) collective-permute-start(f32[200,256]{1,0:T(8,128)S(1)} %get-tuple-element.26), channel_id=1, source_target_pairs={{0,6},{1,7},{2,0},{3,1},{4,2},{5,3},{6,4},{7,5},{8,14},{9,15},{10,... | collective-permute-start | bytes 614408 | tf_op jit(solution)/shard_map/ppermute | solution.py:375
  14.5 9.5 %collective-permute-start.2 = (f32[200,256]{1,0:T(8,128)S(1)}, f32[200,256]{1,0:T(8,128)S(1)}, u32[]{:S(2)}, u32[]{:S(2)}) collective-permute-start(f32[200,256]{1,0:T(8,128)S(1)} %get-tuple-element.26), channel_id=1, source_target_pairs={{0,4},{1,5},{2,6},{3,7},{4,0},{5,1},{6,2},{7,3},{8,12},{9,13},{10,... | collective-permute-start | bytes 614408 | tf_op jit(solution)/shard_map/ppermute | solution.py:375
  15.2 12.1 %collective-permute-start.1 = (f32[200,256]{1,0:T(8,128)S(1)}, f32[200,256]{1,0:T(8,128)S(1)}, u32[]{:S(2)}, u32[]{:S(2)}) collective-permute-start(f32[200,256]{1,0:T(8,128)S(1)} %get-tuple-element.26), channel_id=1, source_target_pairs={{0,2},{1,3},{2,4},{3,5},{4,6},{5,7},{6,0},{7,1},{8,10},{9,11},{10,... | collective-permute-start | bytes 614408 | tf_op jit(solution)/shard_map/ppermute | solution.py:375
  21.2 15.4 %copy-start = (f32[4,256,256]{2,1,0:T(8,128)}, f32[4,256,256]{2,1,0:T(8,128)S(1)}, u32[]{:S(2)}) copy-start(f32[4,256,256]{2,1,0:T(8,128)S(1)} %get-tuple-element.31.refs_3_.refs_9_) | copy-start | bytes 3145732
  23.6 3.8 %collective-permute-start.6 = (f32[200,256]{1,0:T(8,128)S(1)}, f32[200,256]{1,0:T(8,128)S(1)}, u32[]{:S(2)}, u32[]{:S(2)}) collective-permute-start(f32[200,256]{1,0:T(8,128)S(1)} %collective-permute-done.3.refs_2_), channel_id=1, source_target_pairs={{0,1},{1,0},{2,3},{3,2},{4,5},{5,4},{6,7},{7,6},{8,9},{9,8},{10,11... | collective-permute-start | bytes 614408 | tf_op jit(solution)/shard_map/ppermute | solution.py:375
  24.0 3.4 %collective-permute-start.5 = (f32[200,256]{1,0:T(8,128)S(1)}, f32[200,256]{1,0:T(8,128)S(1)}, u32[]{:S(2)}, u32[]{:S(2)}) collective-permute-start(f32[200,256]{1,0:T(8,128)S(1)} %collective-permute-done.2.refs_1_), channel_id=1, source_target_pairs={{0,1},{1,0},{2,3},{3,2},{4,5},{5,4},{6,7},{7,6},{8,9},{9,8},{10,11... | collective-permute-start | bytes 614408 | tf_op jit(solution)/shard_map/ppermute | solution.py:375
  27.3 1.5 %collective-permute-start.4 = (f32[200,256]{1,0:T(8,128)S(1)}, f32[200,256]{1,0:T(8,128)S(1)}, u32[]{:S(2)}, u32[]{:S(2)}) collective-permute-start(f32[200,256]{1,0:T(8,128)S(1)} %pass_y.1), channel_id=1, source_target_pairs={{0,1},{1,0},{2,3},{3,2},{4,5},{5,4},{6,7},{7,6},{8,9},{9,8},{10,11... | collective-permute-start | bytes 614408 | tf_op jit(solution)/shard_map/ppermute | solution.py:375
  31.3 11.9 %collective-permute-start.9 = (f32[200,256]{1,0:T(8,128)S(1)}, f32[200,256]{1,0:T(8,128)S(1)}, u32[]{:S(2)}, u32[]{:S(2)}) collective-permute-start(f32[200,256]{1,0:T(8,128)S(1)} %get-tuple-element.29), channel_id=1, source_target_pairs={{0,24},{1,25},{2,26},{3,27},{4,28},{5,29},{6,30},{7,31},{8,0},{9,1... | collective-permute-start | bytes 614408 | tf_op jit(solution)/shard_map/ppermute | solution.py:375
  34.1 9.5 %collective-permute-start.8 = (f32[200,256]{1,0:T(8,128)S(1)}, f32[200,256]{1,0:T(8,128)S(1)}, u32[]{:S(2)}, u32[]{:S(2)}) collective-permute-start(f32[200,256]{1,0:T(8,128)S(1)} %get-tuple-element.29), channel_id=1, source_target_pairs={{0,16},{1,17},{2,18},{3,19},{4,20},{5,21},{6,22},{7,23},{8,24},{9,... | collective-permute-start | bytes 614408 | tf_op jit(solution)/shard_map/ppermute | solution.py:375
  34.9 11.9 %collective-permute-start.7 = (f32[200,256]{1,0:T(8,128)S(1)}, f32[200,256]{1,0:T(8,128)S(1)}, u32[]{:S(2)}, u32[]{:S(2)}) collective-permute-start(f32[200,256]{1,0:T(8,128)S(1)} %get-tuple-element.29), channel_id=1, source_target_pairs={{0,8},{1,9},{2,10},{3,11},{4,12},{5,13},{6,14},{7,15},{8,16},{9,17... | collective-permute-start | bytes 614408 | tf_op jit(solution)/shard_map/ppermute | solution.py:375
  41.4 14.8 %copy-start.5 = (f32[2,256,256]{2,1,0:T(8,128)}, f32[2,256,256]{2,1,0:T(8,128)S(1)}, u32[]{:S(2)}) copy-start(f32[2,256,256]{2,1,0:T(8,128)S(1)} %get-tuple-element.38.refs_4_.refs_13_) | copy-start | bytes 1572868
  43.2 3.8 %collective-permute-start.12 = (f32[200,256]{1,0:T(8,128)S(1)}, f32[200,256]{1,0:T(8,128)S(1)}, u32[]{:S(2)}, u32[]{:S(2)}) collective-permute-start(f32[200,256]{1,0:T(8,128)S(1)} %collective-permute-done.9.refs_2_), channel_id=1, source_target_pairs={{0,1},{1,0},{2,3},{3,2},{4,5},{5,4},{6,7},{7,6},{8,9},{9,8},{10,11... | collective-permute-start | bytes 614408 | tf_op jit(solution)/shard_map/ppermute | solution.py:375
  43.6 3.4 %collective-permute-start.11 = (f32[200,256]{1,0:T(8,128)S(1)}, f32[200,256]{1,0:T(8,128)S(1)}, u32[]{:S(2)}, u32[]{:S(2)}) collective-permute-start(f32[200,256]{1,0:T(8,128)S(1)} %collective-permute-done.8.refs_1_), channel_id=1, source_target_pairs={{0,1},{1,0},{2,3},{3,2},{4,5},{5,4},{6,7},{7,6},{8,9},{9,8},{10,11... | collective-permute-start | bytes 614408 | tf_op jit(solution)/shard_map/ppermute | solution.py:375
  46.9 1.5 %collective-permute-start.10 = (f32[200,256]{1,0:T(8,128)S(1)}, f32[200,256]{1,0:T(8,128)S(1)}, u32[]{:S(2)}, u32[]{:S(2)}) collective-permute-start(f32[200,256]{1,0:T(8,128)S(1)} %pass_x.1), channel_id=1, source_target_pairs={{0,1},{1,0},{2,3},{3,2},{4,5},{5,4},{6,7},{7,6},{8,9},{9,8},{10,11... | collective-permute-start | bytes 614408 | tf_op jit(solution)/shard_map/ppermute | solution.py:375
  50.9 13.1 %collective-permute-start.15 = (f32[200,256]{1,0:T(8,128)S(1)}, f32[200,256]{1,0:T(8,128)S(1)}, u32[]{:S(2)}, u32[]{:S(2)}) collective-permute-start(f32[200,256]{1,0:T(8,128)S(1)} %ring_x.1.refs_6_), channel_id=1, source_target_pairs={{0,96},{1,97},{2,98},{3,99},{4,100},{5,101},{6,102},{7,103},{8,104... | collective-permute-start | bytes 614408 | tf_op jit(solution)/shard_map/ppermute | solution.py:375
  55.0 9.5 %collective-permute-start.14 = (f32[200,256]{1,0:T(8,128)S(1)}, f32[200,256]{1,0:T(8,128)S(1)}, u32[]{:S(2)}, u32[]{:S(2)}) collective-permute-start(f32[200,256]{1,0:T(8,128)S(1)} %ring_x.1.refs_6_), channel_id=1, source_target_pairs={{0,64},{1,65},{2,66},{3,67},{4,68},{5,69},{6,70},{7,71},{8,72},{9,... | collective-permute-start | bytes 614408 | tf_op jit(solution)/shard_map/ppermute | solution.py:375
  55.0 12.4 %collective-permute-start.13 = (f32[200,256]{1,0:T(8,128)S(1)}, f32[200,256]{1,0:T(8,128)S(1)}, u32[]{:S(2)}, u32[]{:S(2)}) collective-permute-start(f32[200,256]{1,0:T(8,128)S(1)} %ring_x.1.refs_6_), channel_id=1, source_target_pairs={{0,32},{1,33},{2,34},{3,35},{4,36},{5,37},{6,38},{7,39},{8,40},{9,... | collective-permute-start | bytes 614408 | tf_op jit(solution)/shard_map/ppermute | solution.py:375
  60.5 8.5 %copy-start.1 = (f32[4,256,256]{2,1,0:T(8,128)S(1)}, f32[4,256,256]{2,1,0:T(8,128)}, u32[]{:S(2)}) copy-start(f32[4,256,256]{2,1,0:T(8,128)} %copy-done) | copy-start | bytes 3145732
  60.5 8.5 %copy-start.2 = (f32[4,256,256]{2,1,0:T(8,128)S(1)}, f32[4,256,256]{2,1,0:T(8,128)}, u32[]{:S(2)}) copy-start(f32[4,256,256]{2,1,0:T(8,128)} %get-tuple-element.32.refs_4_.refs_10_) | copy-start | bytes 3145732
  60.5 8.5 %copy-start.6 = (f32[2,256,256]{2,1,0:T(8,128)S(1)}, f32[2,256,256]{2,1,0:T(8,128)}, u32[]{:S(2)}) copy-start(f32[2,256,256]{2,1,0:T(8,128)} %copy-done.5) | copy-start | bytes 1572868
  60.5 8.5 %copy-start.7 = (f32[256,256]{1,0:T(8,128)S(1)}, f32[256,256]{1,0:T(8,128)}, u32[]{:S(2)}) copy-start(f32[256,256]{1,0:T(8,128)} %refs_19_.1) | copy-start | bytes 786436
  60.5 8.5 %copy-start.8 = (f32[256]{0:T(256)S(1)}, f32[256]{0:T(256)}, u32[]{:S(2)}) copy-start(f32[256]{0:T(256)} %param.8) | copy-start | bytes 3076
  64.0 3.5 %collective-permute-start.18 = (f32[200,256]{1,0:T(8,128)S(1)}, f32[200,256]{1,0:T(8,128)S(1)}, u32[]{:S(2)}, u32[]{:S(2)}) collective-permute-start(f32[200,256]{1,0:T(8,128)S(1)} %collective-permute-done.15.refs_2_), channel_id=1, source_target_pairs={{0,1},{1,0},{2,3},{3,2},{4,5},{5,4},{6,7},{7,6},{8,9},{9,8},{10,11... | collective-permute-start | bytes 614408 | tf_op jit(solution)/shard_map/ppermute | solution.py:375
  64.4 3.1 %collective-permute-start.17 = (f32[200,256]{1,0:T(8,128)S(1)}, f32[200,256]{1,0:T(8,128)S(1)}, u32[]{:S(2)}, u32[]{:S(2)}) collective-permute-start(f32[200,256]{1,0:T(8,128)S(1)} %collective-permute-done.14.refs_1_), channel_id=1, source_target_pairs={{0,1},{1,0},{2,3},{3,2},{4,5},{5,4},{6,7},{7,6},{8,9},{9,8},{10,11... | collective-permute-start | bytes 614408 | tf_op jit(solution)/shard_map/ppermute | solution.py:375
  67.4 1.5 %collective-permute-start.16 = (f32[200,256]{1,0:T(8,128)S(1)}, f32[200,256]{1,0:T(8,128)S(1)}, u32[]{:S(2)}, u32[]{:S(2)}) collective-permute-start(f32[200,256]{1,0:T(8,128)S(1)} %pass_z.1), channel_id=1, source_target_pairs={{0,1},{1,0},{2,3},{3,2},{4,5},{5,4},{6,7},{7,6},{8,9},{9,8},{10,11... | collective-permute-start | bytes 614408 | tf_op jit(solution)/shard_map/ppermute | solution.py:375
